TPU v7x, 32 devices: a whole 2x2x4 slice. The times are simulated.
32 devices in a mesh: seq: 8 (over z, y), chan: 4 (over x, core).
Axes of the slice: x: 2, y: 2, z: 4, core: 2. Of those that a mesh axis runs over, the one named last changes fastest.
Arguments:
- query_in: bfloat16 [1024, 6144], P('seq', 'chan'), may hold values from -6 to 6
- key_in: bfloat16 [1024, 6144], P('seq', 'chan'), may hold values from -6 to 6
- value_in: bfloat16 [1024, 6144], P('seq', 'chan'), may hold values from -6 to 6
- filters: bfloat16 [384, 128], P('chan'), may hold values from -0.5 to 0.5
- doc_lengths: int32 [16], replicated, may hold values from 1 to 256, 1024 in all
- w_out: bfloat16 [6144, 6144], P('chan'), may hold values from -0.109375 to 0.109375
- cotangent: bfloat16 [1024, 6144], P('seq', 'chan'), may hold values from -6 to 6
Outputs:
- block_out: bfloat16 [1024, 6144], P('seq', 'chan')
- grad_query: bfloat16 [1024, 6144], P('seq', 'chan')
- grad_key: bfloat16 [1024, 6144], P('seq', 'chan')
- grad_value: bfloat16 [1024, 6144], P('seq', 'chan')
- grad_w_out: bfloat16 [6144, 6144], P('chan', 'seq')
- grad_filters: float32 [384, 128], P('chan', 'seq')
Inputs may be any that keep to these rules, and one draw needn't show every extreme that they name: `doc_lengths`: the lengths sum to 1024.
All inputs are finite; a program needn't handle non-finite values.
Results may differ from a plain program's by a relative error of at most 0.02.
Values may be sent and summed in bfloat16 or wider, within the bound.
A program may use at most 128 MiB of HBM per device.

v0:
```python
import jax
import jax.numpy as jnp
from jax import lax
from jax.sharding import PartitionSpec as P


def padded_2(array, sides, width):
    for axis, dim in sides:
        peers, length = (lax.axis_size(axis), array.shape[dim])
        up = [(i, (i + 1) % peers) for i in range(peers - 1)]
        down = [(j, i) for i, j in up]
        last = lax.slice_in_dim(array, length - width, length, axis=dim)
        leading = lax.slice_in_dim(array, 0, width, axis=dim)
        before = lax.ppermute(last, axis, up)
        after = lax.ppermute(leading, axis, down)
        array = jnp.concatenate([before, array, after], axis=dim)
    return array


def doc_start(positions, starts):
    before = starts[None, :] <= positions[:, None]
    return jnp.max(jnp.where(before, starts[None, :], 0), axis=1)


def banded(tap_rows, tok_rows):
    group_count, length = tap_rows.shape
    padded = jnp.concatenate([tap_rows, jnp.zeros((group_count, tok_rows), tap_rows.dtype)], axis=1)
    tiled_taps = jnp.tile(padded, (1, tok_rows))
    return tiled_taps[:, : tok_rows * (tok_rows + length - 1)].reshape(
        group_count, tok_rows, tok_rows + length - 1
    )


def collect(cotangent, w_out):
    shard_piece = lax.all_gather(cotangent, "chan", axis=1, tiled=True)
    grad_in = jnp.einsum("tn,cn->tc", shard_piece, w_out, preferred_element_type=jnp.float32)
    return (grad_in, shard_piece)


def apply_filter(forward_band, mixed_ext, query_in):
    tok_rows, chan_count = query_in.shape
    group_count = forward_band.shape[0]
    grouped = mixed_ext.reshape(mixed_ext.shape[0], group_count, chan_count // group_count)
    filtered = jnp.einsum(
        "gti,igc->tgc", forward_band, grouped, preferred_element_type=jnp.float32
    ).reshape(tok_rows, chan_count)
    gated = (query_in.astype(jnp.float32) * filtered).astype(jnp.bfloat16)
    return (filtered, gated)


def project(gated, w_out):
    partial_out = jnp.dot(gated, w_out, preferred_element_type=jnp.float32)
    return lax.psum_scatter(
        partial_out.astype(jnp.bfloat16), "chan", scatter_dimension=1, tiled=True
    )


def body(query_in, key_in, value_in, filters, doc_lengths, w_out, cotangent):
    tok_rows, chan_count = query_in.shape
    group_count, length = filters.shape
    tap_reach = length - 1
    product_kv = (key_in.astype(jnp.float32) * value_in.astype(jnp.float32)).astype(jnp.bfloat16)
    starts = jnp.cumsum(doc_lengths) - doc_lengths
    first_row = lax.axis_index("seq") * tok_rows
    local_steps = jnp.arange(tok_rows, dtype=jnp.int32)
    wide_steps = jnp.arange(tok_rows + tap_reach, dtype=jnp.int32)
    own_pos = first_row + local_steps
    fwd_mask = (first_row - tap_reach + wide_steps)[None, :] >= doc_start(own_pos, starts)[:, None]
    back_mask = own_pos[:, None] >= doc_start(first_row + wide_steps, starts)[None, :]
    forward_band = banded(jnp.flip(filters, 1), tok_rows) * fwd_mask.astype(jnp.bfloat16)[None]
    backward_band = banded(filters, tok_rows) * back_mask.astype(jnp.bfloat16)[None]
    grad_in, full_cot = collect(cotangent, w_out)
    grad_gate = (grad_in * query_in.astype(jnp.float32)).astype(jnp.bfloat16)
    rims_out = padded_2(jnp.stack([product_kv, grad_gate]), (("seq", 1),), tap_reach)
    mixed_ext = rims_out[0, : tok_rows + tap_reach]
    grad_ext = rims_out[1, tap_reach:]
    filtered, gated = apply_filter(forward_band, mixed_ext, query_in)
    block_out = project(gated, w_out)
    weight_part = jnp.einsum("tc,tn->cn", gated, full_cot, preferred_element_type=jnp.float32)
    grad_query = (grad_in * filtered).astype(jnp.bfloat16)
    per_group = chan_count // group_count
    grad_mixed = jnp.einsum(
        "gtr,rgc->tgc",
        backward_band,
        grad_ext.reshape(tok_rows + tap_reach, group_count, per_group),
        preferred_element_type=jnp.float32,
    ).reshape(tok_rows, chan_count)
    grad_key = (grad_mixed * value_in.astype(jnp.float32)).astype(jnp.bfloat16)
    grad_value = (grad_mixed * key_in.astype(jnp.float32)).astype(jnp.bfloat16)
    pair_terms = jnp.einsum(
        "tgc,igc->gti",
        grad_gate.reshape(tok_rows, group_count, per_group),
        mixed_ext.reshape(tok_rows + tap_reach, group_count, per_group),
        preferred_element_type=jnp.float32,
    )
    pair_terms = pair_terms * fwd_mask.astype(jnp.float32)[None]
    flat_pairs = pair_terms.reshape(group_count, tok_rows * (tok_rows + tap_reach))
    flat_pairs = jnp.concatenate(
        [flat_pairs, jnp.zeros((group_count, tok_rows), jnp.float32)], axis=1
    )
    diagonals = flat_pairs.reshape(group_count, tok_rows, tok_rows + length)[:, :, :length]
    tap_part = jnp.flip(jnp.sum(diagonals, axis=1), 1)
    weight_sum, tap_sum = (
        lax.psum_scatter(
            weight_part.astype(jnp.bfloat16), "seq", scatter_dimension=1, tiled=True
        ).astype(jnp.float32),
        lax.psum_scatter(
            tap_part.astype(jnp.bfloat16), "seq", scatter_dimension=1, tiled=True
        ).astype(jnp.float32),
    )
    return (block_out, grad_query, grad_key, grad_value, weight_sum.astype(jnp.bfloat16), tap_sum)


def solution(mesh):
    return jax.shard_map(
        body,
        mesh=mesh,
        in_specs=(
            P("seq", "chan"),
            P("seq", "chan"),
            P("seq", "chan"),
            P("chan", None),
            P(),
            P("chan", None),
            P("seq", "chan"),
        ),
        out_specs=(
            P("seq", "chan"),
            P("seq", "chan"),
            P("seq", "chan"),
            P("seq", "chan"),
            P("chan", "seq"),
            P("chan", "seq"),
        ),
        check_vma=False,
    )
```

profile of v0, /device:TPU:0, one launch (start us, length us, event | category | flops | bytes accessed | tf_op | source)
XLA Modules:
  0.0 554.2 jit_solution(860209915167474281)
XLA Ops:
  7.2 0.0 all-gather.2.cloned.1.call-start
  7.2 0.7 all-gather.2.cloned.1.call-update
  7.9 0.0 reduce-scatter.10.cloned.1.call-start
  7.9 1.2 fusion.11
  9.2 0.0 copy-start.6
  9.2 0.0 copy-start.4
  9.2 22.8 %all-gather.2.cloned.1.call-done = bf16[128,6144]{1,0:T(8,128)(2,1)} async-done(((bf16[128,1536]{1,0:T(8,128)(2,1)}), bf16[128,6144]{1,0:T(8,128)(2,1)}) %all-gather.2.cloned.1.call-update) | async-done | bytes 1572880 | tf_op jit(solution)/shard_map/all_gather | solution.py:35
  32.0 13.2 %fusion.6 = (bf16[128,1536]{1,0:T(8,128)(2,1)S(1)}, f32[128,1536]{1,0:T(8,128)S(1)}) fusion(bf16[128,1536]{1,0:T(8,128)(2,1)} %param.7, bf16[128,6144]{1,0:T(8,128)(2,1)} %all-gather.2.cloned.1.call-done, bf16[1536,6144]{1,0:T(8,128)(2,1)} %param.12), kind=kOutput, calls=%fused_computation.15 | convolution fusion | flops 2416508928 | bytes 22020096 | tf_op jit(solution)/shard_map/tn,cn->tc/dot_general | solution.py:36
  45.1 0.2 pad_maximum_fusion.2
  45.3 1.7 copy.54
  47.0 3.4 collective-permute-start
  50.4 1.7 copy.60
  52.1 1.8 collective-permute-start.1
  53.9 0.0 copy-done.6
  53.9 0.1 copy.57
  54.1 0.1 reduce
  54.2 0.0 copy-done.4
  54.2 0.1 rev.8
  54.3 0.4 tile.8
  54.7 4.2 copy.69
  58.9 3.1 slice.32
  62.0 22.8 %reshape.160 = bf16[96,128,255]{2,1,0:T(8,128)(2,1)} reshape(bf16[96,32640]{1,0:T(8,128)(2,1)} %slice.32) | data formatting | bytes 12533760 | tf_op jit(solution)/shard_map/reshape | solution.py:29
  84.8 0.1 select_reduce_fusion.1
  84.9 0.8 compare_convert_fusion
  85.7 0.2 copy.65
  85.9 0.0 collective-permute-done
  85.9 0.1 copy.55
  86.0 0.0 collective-permute-done.1
  86.0 1.2 copy.61
  87.2 1.3 pad_maximum_fusion
  88.5 1.4 copy.56
  89.9 4.5 fusion.2
  94.4 0.3 copy.58
  94.7 7.3 %broadcast_multiply_fusion = f32[96,128,255]{2,1,0:T(8,128)} fusion(f32[128,255]{1,0:T(8,128)} %get-tuple-element.30, bf16[128,96,16]{0,2,1:T(8,128)(2,1)S(1)} %bitcast.42, bf16[255,96,16]{0,2,1:T(8,128)(2,1)S(1)} %bitcast.36), kind=kOutput, calls=%fused_computation.3 | convolution fusion | flops 103403520 | bytes 13840896 | tf_op jit(solution)/shard_map/tgc,igc->gti/dot_general | solution.py:90
  102.0 13.5 %reshape.167 = f32[96,32640]{1,0:T(8,128)} reshape(f32[96,128,255]{2,1,0:T(8,128)} %broadcast_multiply_fusion) | data formatting | bytes 25067520 | tf_op jit(solution)/shard_map/reshape | solution.py:97
  115.5 10.3 %concatenate.20 = f32[96,32768]{1,0:T(8,128)} pad(f32[96,32640]{1,0:T(8,128)} %reshape.167, f32[]{:T(128)} %constant.22.clone.1), padding=0_0x0_128 | pad | bytes 25116676 | tf_op jit(solution)/shard_map/concatenate | solution.py:98
  125.9 12.8 %copy.71 = f32[12,8,128,256]{3,2,1,0:T(8,128)} copy(f32[12,8,128,256]{3,1,2,0:T(8,128)} %bitcast.29) | data formatting | bytes 25165824
  138.7 3.6 slice_reduce_fusion
  142.3 0.1 rev.9
  142.4 0.7 copy.67
  143.1 0.0 reduce-scatter.10.cloned.1.call-update
  143.2 0.0 copy-start
  143.2 0.0 reduce-scatter.6.cloned.1.call-start
  143.2 0.0 copy-done.1
  143.2 10.3 %convolution_convert_fusion.1 = bf16[128,6144]{1,0:T(8,128)(2,1)} fusion(bf16[1536,6144]{1,0:T(8,128)(2,1)} %param.12, f32[128,1536]{1,0:T(8,128)S(1)} %copy.58, bf16[128,1536]{1,0:T(8,128)(2,1)S(1)} %copy-done.1), kind=kOutput, calls=%fused_computation.1 | convolution fusion | flops 2417295360 | bytes 21626880 | tf_op jit(solution)/shard_map/dot_general | solution.py:52
  153.5 0.0 reduce-scatter.6.cloned.1.call-update
  153.5 0.0 reduce-scatter.8.cloned.1.call-start
  153.6 9.4 %convolution_convert_fusion = bf16[1536,6144]{1,0:T(8,128)(2,1)} fusion(bf16[128,6144]{1,0:T(8,128)(2,1)S(1)} %copy-done, f32[128,1536]{1,0:T(8,128)S(1)} %copy.58, bf16[128,1536]{1,0:T(8,128)(2,1)S(1)} %copy-done.1), kind=kOutput, calls=%fused_computation | convolution fusion | flops 2425946112 | bytes 21626880 | tf_op jit(solution)/shard_map/tc,tn->cn/dot_general | solution.py:79
  162.9 0.0 reduce-scatter.8.cloned.1.call-update
  163.0 0.7 copy-done.5
  163.7 0.4 tile.20
  164.1 4.2 copy.70
  168.3 3.1 slice.33
  171.4 22.7 %reshape.164 = bf16[96,128,255]{2,1,0:T(8,128)(2,1)} reshape(bf16[96,32640]{1,0:T(8,128)(2,1)} %slice.33) | data formatting | bytes 12533760 | tf_op jit(solution)/shard_map/reshape | solution.py:29
  194.2 0.1 select_reduce_fusion
  194.3 0.7 compare_convert_fusion.2
  195.0 0.3 copy.62
  195.3 5.5 fusion
  200.7 1.4 copy.63
  202.1 2.2 fusion.8
  204.3 0.8 copy.68
  205.1 0.7 copy.66
  205.8 23.4 %reduce-scatter.6.cloned.1.call-done = bf16[128,1536]{1,0:T(8,128)(2,1)} async-done(((bf16[128,6144]{1,0:T(8,128)(2,1)}), bf16[128,1536]{1,0:T(8,128)(2,1)}) %reduce-scatter.6.cloned.1.call-update) | async-done | bytes 393232 | tf_op jit(solution)/shard_map/reduce_scatter | solution.py:53
  229.2 318.2 %reduce-scatter.8.cloned.1.call-done = bf16[1536,768]{1,0:T(8,128)(2,1)} async-done(((bf16[1536,6144]{1,0:T(8,128)(2,1)}), bf16[1536,768]{1,0:T(8,128)(2,1)}) %reduce-scatter.8.cloned.1.call-update) | async-done | bytes 2359312 | tf_op jit(solution)/shard_map/reduce_scatter | solution.py:104
  (15 shorter events, 0.1 us)
Async XLA Ops:
  7.2 24.8 %all-gather.2.cloned.1.call-start = ((), (), s32[]{:S(2)}) async-start(), calls=%async_computation.3 | async-start | bytes 1966080 | tf_op jit(solution)/shard_map/all_gather | solution.py:35
  7.9 196.4 %reduce-scatter.10.cloned.1.call-start = ((), (), s32[]{:S(2)}) async-start(), calls=%async_computation.6 | async-start | bytes 36864
  9.2 44.8 %copy-start.6 = (s32[16]{0:T(128)S(1)}, s32[16]{0:T(128)}, u32[]{:S(2)}) copy-start(s32[16]{0:T(128)} %param.11) | copy-start | bytes 196
  9.2 45.0 %copy-start.4 = (bf16[96,128]{1,0:T(8,128)(2,1)S(1)}, bf16[96,128]{1,0:T(8,128)(2,1)}, u32[]{:S(2)}) copy-start(bf16[96,128]{1,0:T(8,128)(2,1)} %param.10) | copy-start | bytes 73732
  47.0 38.9 %collective-permute-start = (bf16[2,127,1536]{2,0,1:T(2,128)(2,1)}, bf16[2,127,1536]{2,0,1:T(2,128)(2,1)S(1)}, u32[]{:S(2)}, u32[]{:S(2)}) collective-permute-start(bf16[2,127,1536]{2,0,1:T(2,128)(2,1)} %copy.54), channel_id=1, source_target_pairs={{0,4},{4,8},{8,12},{12,16},{16,20},{20,24},{24,28},{1,5},{5,9},{9,... | collective-permute-start | bytes 2340872 | tf_op jit(solution)/shard_map/ppermute | solution.py:14
  52.1 33.9 %collective-permute-start.1 = (bf16[2,127,1536]{2,0,1:T(2,128)(2,1)}, bf16[2,127,1536]{2,0,1:T(2,128)(2,1)}, u32[]{:S(2)}, u32[]{:S(2)}) collective-permute-start(bf16[2,127,1536]{2,0,1:T(2,128)(2,1)} %copy.60), channel_id=1, source_target_pairs={{4,0},{8,4},{12,8},{16,12},{20,16},{24,20},{28,24},{5,1},{9,5},{13... | collective-permute-start | bytes 2340872 | tf_op jit(solution)/shard_map/ppermute | solution.py:15
  138.7 4.5 copy-start.1
  143.2 10.4 %copy-start = (bf16[128,6144]{1,0:T(8,128)(2,1)S(1)}, bf16[128,6144]{1,0:T(8,128)(2,1)}, u32[]{:S(2)}) copy-start(bf16[128,6144]{1,0:T(8,128)(2,1)} %all-gather.2.cloned.1.call-done) | copy-start | bytes 4718596
  143.2 86.0 %reduce-scatter.6.cloned.1.call-start = ((), (), s32[]{:S(2)}) async-start(), calls=%async_computation.4 | async-start | bytes 1966080 | tf_op jit(solution)/shard_map/reduce_scatter | solution.py:53
  153.5 393.9 %reduce-scatter.8.cloned.1.call-start = ((), (), s32[]{:S(2)}) async-start(), calls=%async_computation.5 | async-start | bytes 21233664 | tf_op jit(solution)/shard_map/reduce_scatter | solution.py:104
  162.9 0.7 copy-start.5
  171.4 23.5 %copy-start.2 = (bf16[1,255,1536]{2,1,0:T(8,128)(2,1)S(1)}, bf16[1,255,1536]{2,1,0:T(8,128)(2,1)}, u32[]{:S(2)}) copy-start(bf16[1,255,1536]{2,1,0:T(8,128)(2,1)} %get-tuple-element.26) | copy-start | bytes 2350084
  194.2 8.0 %copy-start.3 = (bf16[128,1536]{1,0:T(8,128)(2,1)S(1)}, bf16[128,1536]{1,0:T(8,128)(2,1)}, u32[]{:S(2)}) copy-start(bf16[128,1536]{1,0:T(8,128)(2,1)} %param.9) | copy-start | bytes 1179652
Sparse Core Ops, SparseCore 0:
  9.6 22.3 all-gather.1
  143.3 55.4 reduce-scatter.9
  201.9 27.2 reduce-scatter.5
  234.0 313.3 reduce-scatter.7
where the time goes:
time: 560 us; the launch traced here: 554 us
  waiting for transfers between devices  365 us (65%)
  local copies, waits for them, and re-layouts  109 us (19%)
  matrix products  50.1 us (9%)
  between operations  14.2 us (3%)
  other arithmetic  10.3 us (2%)
    reduce_scatter x1, waiting for transfers between devices, body(): lax.psum_scatter(weight_part.astype(jnp.bfloat16), 'seq', scatter_dimensi...  318 us
    reshape x2, local copies, waits for them, and re-layouts, banded(): tiled_taps[:, :tok_rows * (tok_rows + length - 1)]  45.5 us
    unnamed x20, local copies, waits for them, and re-layouts  24.2 us
    reduce_scatter x1, waiting for transfers between devices, project(): lax.psum_scatter(partial_out.astype(jnp.bfloat16), 'chan', scatter_dimens...  23.4 us
    all_gather x1, waiting for transfers between devices, collect(): shard_piece = lax.all_gather(cotangent, 'chan', axis=1, tiled=True)  22.8 us
    reshape x1, local copies, waits for them, and re-layouts, body(): pair_terms.reshape(group_count, tok_rows * (tok_rows + tap_reach))  13.5 us
    dot_general x1, matrix products, collect(): jnp.einsum('tn,cn->tc', shard_piece, w_out, preferred_element_type=jnp.fl...  13.2 us
  transfers between devices with their start and end apart: 6, of which 3 were waited for; matrix products, arithmetic and copies ran while one was open for 17% of the time, Pallas kernels for 0%

commit v1 on v0

v1 whole, which is shorter than its diff:
```python
import functools

import jax
import jax.numpy as jnp
from jax import lax
from jax.experimental import pallas as pl
from jax.experimental.pallas import tpu as pltpu
from jax.sharding import PartitionSpec as P

F32 = jnp.float32
BF16 = jnp.bfloat16
LANES = 128


def doc_start(positions, starts):
    before = starts[None, :] <= positions[:, None]
    return jnp.max(jnp.where(before, starts[None, :], 0), axis=1)


def toeplitz(row, rows):
    wide = jnp.broadcast_to(row, (rows, row.shape[-1]))
    return pltpu.roll(wide, 0, 1, stride=1, stride_axis=0)


def group_lanes(rows, per_group, index):
    lane = lax.broadcasted_iota(jnp.int32, (rows, LANES), 1)
    return (lane >= index * per_group) & (lane < (index + 1) * per_group)


def forward_kernel(per_group, q_ref, prev_ref, own_ref, taps_ref, mask_ref, filt_ref, gated_ref):
    rows, width = q_ref.shape
    mask = mask_ref[...].astype(F32)
    per_tile = LANES // per_group
    for tile in range(width // LANES):
        cols = slice(tile * LANES, (tile + 1) * LANES)
        ext = jnp.concatenate([prev_ref[:, cols], own_ref[:, cols]], axis=0)
        acc = jnp.zeros((rows, LANES), F32)
        for g in range(per_tile):
            row = tile * per_tile + g
            band = (toeplitz(taps_ref[row : row + 1, :], rows) * mask).astype(BF16)
            res = jnp.dot(band, ext, preferred_element_type=F32)
            acc = jnp.where(group_lanes(rows, per_group, g), res, acc)
        filt_ref[:, cols] = acc
        gated_ref[:, cols] = (q_ref[:, cols].astype(F32) * acc).astype(BF16)


def backward_kernel(
    per_group, k_ref, v_ref, prev_ref, own_ref, gate_ref, next_ref, grad_in_ref, filt_ref, taps_ref,
    fmask_ref, bmask_ref, gq_ref, gk_ref, gv_ref, sums_ref,
):
    rows, width = k_ref.shape
    bmask = bmask_ref[...].astype(F32)
    fmask = fmask_ref[...].astype(F32)
    per_tile = LANES // per_group
    r = lax.broadcasted_iota(jnp.int32, (rows, rows), 0)
    c = lax.broadcasted_iota(jnp.int32, (rows, rows), 1)
    flip = jnp.where(r + c == rows - 1, 1.0, 0.0).astype(BF16)
    gq_ref[...] = (grad_in_ref[...] * filt_ref[...]).astype(BF16)
    for tile in range(width // LANES):
        cols = slice(tile * LANES, (tile + 1) * LANES)
        gate = gate_ref[:, cols]
        gext = jnp.concatenate([gate, next_ref[:, cols]], axis=0)
        ext = jnp.concatenate([prev_ref[:, cols], own_ref[:, cols]], axis=0)
        turned = jnp.dot(flip, gate, preferred_element_type=F32)
        acc = jnp.zeros((rows, LANES), F32)
        for g in range(per_tile):
            row = tile * per_tile + g
            lanes = group_lanes(rows, per_group, g)
            band = (toeplitz(taps_ref[row : row + 1, :], rows) * bmask).astype(BF16)
            res = jnp.dot(band, gext, preferred_element_type=F32)
            acc = jnp.where(lanes, res, acc)
            mine = jnp.where(lanes, turned, 0.0).astype(BF16)
            pair = lax.dot_general(
                mine, ext, (((1,), (1,)), ((), ())), preferred_element_type=F32
            )
            pair = pltpu.roll(pair * fmask, 0, 1, stride=1, stride_axis=0)
            sums_ref[row : row + 1, :] = jnp.sum(pair, axis=0, keepdims=True)
        gk_ref[:, cols] = (acc * v_ref[:, cols].astype(F32)).astype(BF16)
        gv_ref[:, cols] = (acc * k_ref[:, cols].astype(F32)).astype(BF16)


def body(n_seq, query_in, key_in, value_in, filters, doc_lengths, w_out, cotangent):
    tok_rows, chan_count = query_in.shape
    group_count, length = filters.shape
    per_group = chan_count // group_count
    step = 2 * LANES if chan_count % (2 * LANES) == 0 else LANES
    step_groups = step // per_group
    span = 2 * tok_rows

    full_cot = lax.all_gather(cotangent, "chan", axis=1, tiled=True)

    product_kv = (key_in.astype(F32) * value_in.astype(F32)).astype(BF16)
    up = [(i, i + 1) for i in range(n_seq - 1)]
    down = [(i + 1, i) for i in range(n_seq - 1)]
    prev_kv = lax.ppermute(product_kv, "seq", up)

    starts = jnp.cumsum(doc_lengths) - doc_lengths
    first_row = lax.axis_index("seq") * tok_rows
    wide = jnp.arange(span, dtype=jnp.int32)
    own_pos = first_row + wide[:tok_rows]
    fmask = ((first_row - tok_rows + wide)[None, :] >= doc_start(own_pos, starts)[:, None]).astype(BF16)
    bmask = (own_pos[:, None] >= doc_start(first_row + wide, starts)[None, :]).astype(BF16)
    taps = filters.astype(F32)
    none = jnp.zeros((group_count, span - length), F32)
    back_taps = jnp.concatenate([taps, none], axis=1)
    fore_taps = jnp.roll(jnp.flip(back_taps, 1), tok_rows + 1, axis=1)

    tile = pl.BlockSpec((tok_rows, step), lambda i: (0, i))
    rowspec = pl.BlockSpec((step_groups, span), lambda i: (i, 0))
    whole = pl.BlockSpec((tok_rows, span), lambda i: (0, 0))
    blocks = chan_count // step
    filtered, gated = pl.pallas_call(
        functools.partial(forward_kernel, per_group),
        grid=(blocks,),
        in_specs=[tile, tile, tile, rowspec, whole],
        out_specs=[tile, tile],
        out_shape=[
            jax.ShapeDtypeStruct((tok_rows, chan_count), F32),
            jax.ShapeDtypeStruct((tok_rows, chan_count), BF16),
        ],
    )(query_in, prev_kv, product_kv, fore_taps, fmask)

    gated_all = lax.all_gather(gated, "seq", axis=0, tiled=True)

    grad_in = jnp.einsum("tn,cn->tc", full_cot, w_out, preferred_element_type=F32)
    grad_gate = (grad_in * query_in.astype(F32)).astype(BF16)
    next_gate = lax.ppermute(grad_gate, "seq", down)
    cot_cols = lax.all_to_all(full_cot, "seq", split_axis=1, concat_axis=0, tiled=True)

    partial_out = jnp.dot(gated, w_out, preferred_element_type=F32)
    block_out = lax.psum_scatter(
        partial_out.astype(BF16), "chan", scatter_dimension=1, tiled=True
    )

    grad_query, grad_key, grad_value, sums = pl.pallas_call(
        functools.partial(backward_kernel, per_group),
        grid=(blocks,),
        in_specs=[tile] * 8 + [rowspec, whole, whole],
        out_specs=[tile] * 3 + [rowspec],
        out_shape=[jax.ShapeDtypeStruct((tok_rows, chan_count), BF16)] * 3
        + [jax.ShapeDtypeStruct((group_count, span), F32)],
    )(
        key_in, value_in, prev_kv, product_kv, grad_gate, next_gate, grad_in, filtered,
        back_taps, jnp.flip(fmask, 0), bmask,
    )
    tap_part = jnp.flip(sums[:, span - length :], 1)
    tap_sum = lax.psum_scatter(
        tap_part.astype(BF16), "seq", scatter_dimension=1, tiled=True
    ).astype(F32)

    weight = lax.dot_general(
        gated_all, cot_cols, (((0,), (0,)), ((), ())), preferred_element_type=F32
    ).astype(BF16)
    return (block_out, grad_query, grad_key, grad_value, weight, tap_sum)


def solution(mesh):
    act = P("seq", "chan")
    return jax.shard_map(
        functools.partial(body, mesh.shape["seq"]),
        mesh=mesh,
        in_specs=(act, act, act, P("chan", None), P(), P("chan", None), act),
        out_specs=(act, act, act, act, P("chan", "seq"), P("chan", "seq")),
        check_vma=False,
    )
```

time: 560 us -> 239 us (0.43)
  waiting for transfers between devices: 365 us -> 151 us
  local copies, waits for them, and re-layouts: 109 us -> 9.56 us
  matrix products: 50.1 us -> 30.3 us
  Pallas kernels: 0 us -> 17.6 us
  starting transfers between devices: 5.38 us -> 12.1 us
  other arithmetic: 10.3 us -> 3.74 us
    reduce_scatter x2 -> x1, waiting for transfers between devices: 342 us -> 23.8 us  [body(): lax.psum_scatter(partial_out.astype(BF16), 'chan', scatter_dimension=1, t...]
    reshape x5 -> x0, local copies, waits for them, and re-layouts: 60.7 us -> none  [the longest x2 45.5 us: banded(): tiled_taps[:, :tok_rows * (tok_rows + length - 1)]]
    all_gather x1 -> x2, waiting for transfers between devices: 22.8 us -> 74.2 us  [the longest x1 59.6 us: body(): gated_all = lax.all_gather(gated, 'seq', axis=0, tiled=True)]
    unnamed x5, waiting for transfers between devices: 0.73 us -> 51.4 us
    dot_general x6 -> x3, matrix products: 50.1 us -> 30.3 us  [the longest x1 14.1 us: body(): jnp.einsum('tn,cn->tc', full_cot, w_out, preferred_element_type=F32)]
    unnamed x20, local copies, waits for them, and re-layouts: 24.2 us -> 5.9 us
    pallas_call x0 -> x2, Pallas kernels: none -> 17.6 us  [the longest x1 10.8 us: body(): pl.pallas_call(functools.partial(backward_kernel, per_group), grid=(block...]
    slice x6 -> x1, local copies, waits for them, and re-layouts: 11.2 us -> 0.8 us  [body(): tap_part = jnp.flip(sums[:, span - length:], 1)]
  transfers between devices with their start and end apart: 6 -> 7, of which waited for: 3 -> 5; matrix products, arithmetic and copies ran while one was open for 17% -> 16% of each run, Pallas kernels for 0% -> 3%
where the time goes in v1:
time: 239 us
  waiting for transfers between devices  151 us (63%)
  matrix products  30.3 us (13%)
  Pallas kernels  17.6 us (7%)
  between operations  13.9 us (6%)
  starting transfers between devices  12.1 us (5%)
  local copies, waits for them, and re-layouts  9.56 us (4%)
  other arithmetic  3.74 us (2%)
    all_gather x1, waiting for transfers between devices, body(): gated_all = lax.all_gather(gated, 'seq', axis=0, tiled=True)  59.6 us
    unnamed x5, waiting for transfers between devices  51.4 us
    reduce_scatter x1, waiting for transfers between devices, body(): lax.psum_scatter(partial_out.astype(BF16), 'chan', scatter_dimension=1, t...  23.8 us
    all_gather x1, waiting for transfers between devices, body(): full_cot = lax.all_gather(cotangent, 'chan', axis=1, tiled=True)  14.7 us
    dot_general x1, matrix products, body(): jnp.einsum('tn,cn->tc', full_cot, w_out, preferred_element_type=F32)  14.1 us
    pallas_call x1, Pallas kernels, body(): pl.pallas_call(functools.partial(backward_kernel, per_group), grid=(block...  10.8 us
    dot_general x1, matrix products, body(): partial_out = jnp.dot(gated, w_out, preferred_element_type=F32)  10.2 us
    pallas_call x1, Pallas kernels, body(): pl.pallas_call(functools.partial(forward_kernel, per_group), grid=(blocks...  6.77 us
  transfers between devices with their start and end apart: 7, of which 5 were waited for; matrix products, arithmetic and copies ran while one was open for 16% of the time, Pallas kernels for 3%

profile of v1, /device:TPU:0, one launch (start us, length us, event | category | flops | bytes accessed | tf_op | source)
XLA Modules:
  0.0 238.5 jit_solution(6122229490415107391)
XLA Ops:
  7.2 0.0 all-gather.3.cloned.1.call-start
  7.2 1.9 copy.26
  9.1 0.0 all-gather.3.cloned.1.call-update
  9.2 0.0 reduce-scatter.7.cloned.1.call-start
  9.2 1.2 multiply_convert_fusion.1.own_ref
  10.4 0.0 copy-start
  10.4 4.9 %collective-permute-start = (bf16[128,1536]{1,0:T(8,128)(2,1)S(1)}, bf16[128,1536]{1,0:T(8,128)(2,1)S(1)}, u32[]{:S(2)}, u32[]{:S(2)}) collective-permute-start(bf16[128,1536]{1,0:T(8,128)(2,1)S(1)} %multiply_convert_fusion.1.own_ref), channel_id=1, source_target_pairs={{0,4},{4,8},{8,12},{12,16},{16,20},{20,24},{24,28},{1,5},{5,9},{9,... | collective-permute-start | bytes 1179656 | tf_op jit(solution)/shard_map/ppermute | solution.py:95
  15.3 0.7 copy.25
  16.1 0.1 reduce
  16.2 0.7 sub.7
  16.9 0.1 select_reduce_fusion.1
  17.0 0.7 pad_convert_fusion.taps_ref
  17.7 0.0 copy-start.4
  17.7 0.1 compare_convert_fusion.1.mask_ref
  17.8 0.0 copy-start.5
  17.8 14.7 %all-gather.3.cloned.1.call-done = bf16[128,6144]{0,1:T(8,128)(2,1)} async-done(((bf16[128,1536]{0,1:T(8,128)(2,1)}), bf16[128,6144]{0,1:T(8,128)(2,1)}) %all-gather.3.cloned.1.call-update) | async-done | bytes 1572880 | tf_op jit(solution)/shard_map/all_gather | solution.py:90
  32.5 14.1 %multiply_convert_fusion = (bf16[128,1536]{1,0:T(8,128)(2,1)S(1)}, f32[128,1536]{1,0:T(8,128)}) fusion(bf16[128,1536]{1,0:T(8,128)(2,1)} %q_ref.1, bf16[128,6144]{0,1:T(8,128)(2,1)} %all-gather.3.cloned.1.call-done, bf16[1536,6144]{1,0:T(8,128)(2,1)} %param.12), kind=kOutput, calls=%fused_computation.2 | convolution fusion | flops 2416508928 | bytes 22020096 | tf_op jit(solution)/shard_map/tn,cn->tc/dot_general | solution.py:125
  46.6 0.0 copy-done
  46.6 0.0 copy-start.3
  46.6 1.3 collective-permute-start.1
  47.9 0.0 copy-done.4
  48.0 0.2 reverse.2
  48.1 0.1 slice.22
  48.2 0.0 copy-done.5
  48.2 0.7 rev.10.fmask_ref
  48.9 0.6 concatenate.11.taps_ref
  49.6 0.1 select_reduce_fusion
  49.7 0.7 compare_convert_fusion.bmask_ref
  50.4 0.0 collective-permute-done.prev_ref
  50.4 0.0 copy-start.2
  50.4 0.7 copy-done.2
  51.1 6.8 %shard_map.118 = (f32[128,1536]{1,0:T(8,128)}, bf16[128,1536]{1,0:T(8,128)(2,1)}) custom-call(bf16[128,1536]{1,0:T(8,128)(2,1)} %q_ref.1, bf16[128,1536]{1,0:T(8,128)(2,1)} %copy-done.2, bf16[128,1536]{1,0:T(8,128)(2,1)} %copy-done, f32[96,256]{1,0:T(8,128)} %concatenate.11.taps_ref, bf16[128,256]{1,0:T(8,128)(2,1)} %copy-done.5), custom_call_target="tpu_custom_call" | custom-call | tf_op jit(solution)/shard_map/pallas_call | solution.py:112
  57.9 1.9 collective-permute-done.1.next_ref
  59.8 0.0 copy-start.6
  59.8 0.0 copy-done.3
  59.8 0.8 copy-done.6
  60.5 0.0 copy-start.1
  60.5 10.8 %shard_map.119 = (bf16[128,1536]{1,0:T(8,128)(2,1)}, bf16[128,1536]{1,0:T(8,128)(2,1)}, bf16[128,1536]{1,0:T(8,128)(2,1)}, f32[96,256]{1,0:T(8,128)}) custom-call(bf16[128,1536]{1,0:T(8,128)(2,1)} %k_ref.1, bf16[128,1536]{1,0:T(8,128)(2,1)} %v_ref.1, bf16[128,1536]{1,0:T(8,128)(2,1)} %copy-done.2, bf16[128,1536]{1,0:T(8,128)(2,1)} %copy-done, ...), custom_call_target="tpu_custom_call" | custom-call | tf_op jit(solution)/shard_map/pallas_call | solution.py:135
  71.4 0.8 slice.19
  72.2 0.1 rev.11
  72.3 0.7 copy.29
  73.0 0.0 reduce-scatter.7.cloned.1.call-update
  73.0 0.0 all-gather.5.cloned.1.call-start
  73.1 0.7 all-gather.5.cloned.1.call-update
  73.8 5.6 %all-to-all-start = ((bf16[128,8,768]{0,2,1:T(8,128)(2,1)}), bf16[128,8,768]{0,2,1:T(8,128)(2,1)S(1)}, u32[]{:S(2)}, u32[]{:S(2)}) async-start(bf16[128,8,768]{0,2,1:T(8,128)(2,1)} %bitcast.1), calls=%async_computation.1 | async-start | bytes 3145728 | tf_op jit(solution)/shard_map/all_to_all | solution.py:128
  79.3 0.2 reduce-scatter.5.cloned.1.call-start
  79.6 0.0 copy-done.1
  79.6 10.2 %convolution_convert_fusion = bf16[128,6144]{1,0:T(8,128)(2,1)} fusion(bf16[128,1536]{1,0:T(8,128)(2,1)S(1)} %copy-done.1, bf16[1536,6144]{1,0:T(8,128)(2,1)} %param.12), kind=kOutput, calls=%fused_computation | convolution fusion | flops 2416705536 | bytes 20840448 | tf_op jit(solution)/shard_map/dot_general | solution.py:130
  89.8 0.0 reduce-scatter.5.cloned.1.call-update
  89.8 50.7 %reduce-scatter.7.cloned.1.call-done = bf16[16,96]{1,0:T(8,128)(2,1)} async-done(((bf16[128,96]{1,0:T(8,128)(2,1)}), bf16[16,96]{1,0:T(8,128)(2,1)}) %reduce-scatter.7.cloned.1.call-update) | async-done | bytes 3088
  140.5 0.8 copy.30
  141.3 0.7 copy.28
  141.9 0.0 all-to-all-done
  141.9 0.7 copy.27
  142.6 59.6 %all-gather.5.cloned.1.call-done = bf16[1024,1536]{1,0:T(8,128)(2,1)} async-done(((bf16[128,1536]{1,0:T(8,128)(2,1)}), bf16[1024,1536]{1,0:T(8,128)(2,1)}) %all-gather.5.cloned.1.call-update) | async-done | bytes 3145744 | tf_op jit(solution)/shard_map/all_gather | solution.py:123
  202.2 6.0 %convolution_convert_fusion.1 = bf16[1536,768]{1,0:T(8,128)(2,1)} fusion(bf16[1024,1536]{1,0:T(8,128)(2,1)} %all-gather.5.cloned.1.call-done, bf16[1024,768]{1,0:T(8,128)(2,1)S(1)} %bitcast.15), kind=kOutput, calls=%fused_computation.1 | convolution fusion | flops 2417098752 | bytes 7077888 | tf_op jit(solution)/shard_map/dot_general | solution.py:151
  208.2 23.8 %reduce-scatter.5.cloned.1.call-done = bf16[128,1536]{1,0:T(8,128)(2,1)} async-done(((bf16[128,6144]{1,0:T(8,128)(2,1)}), bf16[128,1536]{1,0:T(8,128)(2,1)}) %reduce-scatter.5.cloned.1.call-update) | async-done | bytes 393232 | tf_op jit(solution)/shard_map/reduce_scatter | solution.py:131
  (5 shorter events, 0.1 us)
Async XLA Ops:
  7.2 25.4 %all-gather.3.cloned.1.call-start = ((), (), s32[]{:S(2)}) async-start(), calls=%async_computation.4 | async-start | bytes 1966080 | tf_op jit(solution)/shard_map/all_gather | solution.py:90
  9.2 131.3 %reduce-scatter.7.cloned.1.call-start = ((), (), s32[]{:S(2)}) async-start(), calls=%async_computation.6 | async-start | bytes 36864
  10.4 36.2 %copy-start = (bf16[128,1536]{1,0:T(8,128)(2,1)}, bf16[128,1536]{1,0:T(8,128)(2,1)S(1)}, u32[]{:S(2)}) copy-start(bf16[128,1536]{1,0:T(8,128)(2,1)S(1)} %multiply_convert_fusion.1.own_ref) | copy-start | bytes 1179652
  10.4 40.0 %collective-permute-start = (bf16[128,1536]{1,0:T(8,128)(2,1)S(1)}, bf16[128,1536]{1,0:T(8,128)(2,1)S(1)}, u32[]{:S(2)}, u32[]{:S(2)}) collective-permute-start(bf16[128,1536]{1,0:T(8,128)(2,1)S(1)} %multiply_convert_fusion.1.own_ref), channel_id=1, source_target_pairs={{0,4},{4,8},{8,12},{12,16},{16,20},{20,24},{24,28},{1,5},{5,9},{9,... | collective-permute-start | bytes 1179656 | tf_op jit(solution)/shard_map/ppermute | solution.py:95
  17.7 30.2 %copy-start.4 = (f32[96,256]{1,0:T(8,128)}, f32[96,256]{1,0:T(8,128)S(1)}, u32[]{:S(2)}) copy-start(f32[96,256]{1,0:T(8,128)S(1)} %pad_convert_fusion.taps_ref) | copy-start | bytes 294916
  17.8 30.4 %copy-start.5 = (bf16[128,256]{1,0:T(8,128)(2,1)}, bf16[128,256]{1,0:T(8,128)(2,1)S(1)}, u32[]{:S(2)}) copy-start(bf16[128,256]{1,0:T(8,128)(2,1)S(1)} %compare_convert_fusion.1.mask_ref) | copy-start | bytes 196612
  46.6 13.1 %copy-start.3 = (bf16[128,1536]{1,0:T(8,128)(2,1)}, bf16[128,1536]{1,0:T(8,128)(2,1)S(1)}, u32[]{:S(2)}) copy-start(bf16[128,1536]{1,0:T(8,128)(2,1)S(1)} %get-tuple-element.48.gate_ref) | copy-start | bytes 1179652
  46.6 13.1 %collective-permute-start.1 = (bf16[128,1536]{1,0:T(8,128)(2,1)S(1)}, bf16[128,1536]{1,0:T(8,128)(2,1)S(1)}, u32[]{:S(2)}, u32[]{:S(2)}) collective-permute-start(bf16[128,1536]{1,0:T(8,128)(2,1)S(1)} %get-tuple-element.48.gate_ref), channel_id=1, source_target_pairs={{4,0},{8,4},{12,8},{16,12},{20,16},{24,20},{28,24},{5,1},{9,5},{13... | collective-permute-start | bytes 1179656 | tf_op jit(solution)/shard_map/ppermute | solution.py:127
  50.4 0.7 copy-start.2
  59.8 0.8 copy-start.6
  60.5 19.0 %copy-start.1 = (bf16[128,1536]{1,0:T(8,128)(2,1)S(1)}, bf16[128,1536]{1,0:T(8,128)(2,1)}, u32[]{:S(2)}) copy-start(bf16[128,1536]{1,0:T(8,128)(2,1)} %get-tuple-element.12) | copy-start | bytes 1179652
  73.0 129.2 %all-gather.5.cloned.1.call-start = ((), (), s32[]{:S(2)}) async-start(), calls=%async_computation.5 | async-start | bytes 3538944 | tf_op jit(solution)/shard_map/all_gather | solution.py:123
  73.8 68.2 %all-to-all-start = ((bf16[128,8,768]{0,2,1:T(8,128)(2,1)}), bf16[128,8,768]{0,2,1:T(8,128)(2,1)S(1)}, u32[]{:S(2)}, u32[]{:S(2)}) async-start(bf16[128,8,768]{0,2,1:T(8,128)(2,1)} %bitcast.1), calls=%async_computation.1 | async-start | bytes 3145728 | tf_op jit(solution)/shard_map/all_to_all | solution.py:128
  79.3 152.7 %reduce-scatter.5.cloned.1.call-start = ((), (), s32[]{:S(2)}) async-start(), calls=%async_computation.3 | async-start | bytes 1966080 | tf_op jit(solution)/shard_map/reduce_scatter | solution.py:131
Sparse Core Ops, SparseCore 0:
  10.1 22.3 all-gather.2
  73.2 67.2 reduce-scatter.6
  142.7 59.4 all-gather.4
  205.2 26.7 reduce-scatter.4

commit v2 on v1

--- a/solution.py
+++ b/solution.py
@@ -79,21 +79,9 @@
         gv_ref[:, cols] = (acc * k_ref[:, cols].astype(F32)).astype(BF16)
 
 
-def body(n_seq, query_in, key_in, value_in, filters, doc_lengths, w_out, cotangent):
-    tok_rows, chan_count = query_in.shape
+def prepare(tok_rows, filters, doc_lengths):
     group_count, length = filters.shape
-    per_group = chan_count // group_count
-    step = 2 * LANES if chan_count % (2 * LANES) == 0 else LANES
-    step_groups = step // per_group
     span = 2 * tok_rows
-
-    full_cot = lax.all_gather(cotangent, "chan", axis=1, tiled=True)
-
-    product_kv = (key_in.astype(F32) * value_in.astype(F32)).astype(BF16)
-    up = [(i, i + 1) for i in range(n_seq - 1)]
-    down = [(i + 1, i) for i in range(n_seq - 1)]
-    prev_kv = lax.ppermute(product_kv, "seq", up)
-
     starts = jnp.cumsum(doc_lengths) - doc_lengths
     first_row = lax.axis_index("seq") * tok_rows
     wide = jnp.arange(span, dtype=jnp.int32)
@@ -104,7 +92,25 @@
     none = jnp.zeros((group_count, span - length), F32)
     back_taps = jnp.concatenate([taps, none], axis=1)
     fore_taps = jnp.roll(jnp.flip(back_taps, 1), tok_rows + 1, axis=1)
-
+    return fore_taps, back_taps, fmask, bmask
+
+
+def body(n_seq, query_in, key_in, value_in, filters, doc_lengths, w_out, cotangent):
+    tok_rows, chan_count = query_in.shape
+    group_count, length = filters.shape
+    per_group = chan_count // group_count
+    step = 2 * LANES if chan_count % (2 * LANES) == 0 else LANES
+    step_groups = step // per_group
+    span = 2 * tok_rows
+
+    full_cot = lax.all_gather(cotangent, "chan", axis=1, tiled=True)
+
+    product_kv = (key_in.astype(F32) * value_in.astype(F32)).astype(BF16)
+    up = [(i, i + 1) for i in range(n_seq - 1)]
+    down = [(i + 1, i) for i in range(n_seq - 1)]
+    prev_kv = lax.ppermute(product_kv, "seq", up)
+
+    fore_taps, back_taps, fmask, bmask = prepare(tok_rows, filters, doc_lengths)
     tile = pl.BlockSpec((tok_rows, step), lambda i: (0, i))
     rowspec = pl.BlockSpec((step_groups, span), lambda i: (i, 0))
     whole = pl.BlockSpec((tok_rows, span), lambda i: (0, 0))
@@ -154,10 +160,406 @@
     return (block_out, grad_query, grad_key, grad_value, weight, tap_sum)
 
 
+def mega_kernel(
+    per_group, n_seq, n_chan, q_ref, k_ref, v_ref, cot_ref, fore_ref, back_ref, fmask_ref, rmask_ref,
+    bmask_ref, w_hbm, out_ref, gq_ref, gk_ref, gv_ref, gw_ref, tap_ref,
+    w_ref, kv_ref, prev_ref, gate_ref, next_ref, filt_ref, gin_ref, gall_ref, cots_ref, cotc_ref,
+    psend_ref, precv_ref, tsend_ref, trecv_ref, sums_ref,
+    w_sem, rim_send, rim_recv, cot_send, cot_recv, part_send, part_recv, a2a_send, a2a_recv,
+    share_send, share_recv, tap_send, tap_recv, line_send, line_recv, pair_send, pair_recv,
+):
+    rows, width = q_ref.shape
+    block = gw_ref.shape[1]
+    per_chan = width // block
+    half = rows // 2
+    tiles = width // LANES
+    per_tile = LANES // per_group
+    s = lax.axis_index("seq")
+    c = lax.axis_index("chan")
+    hops = n_seq // 2
+    z = s // 2
+    pair = s + 1 - 2 * (s % 2)
+    mate = c + 1 - 2 * (c % 2)
+    core = c % 2
+
+    def remote(src, dst, send, recv, seq, chan):
+        return pltpu.make_async_remote_copy(
+            src_ref=src, dst_ref=dst, send_sem=send, recv_sem=recv,
+            device_id=(seq, chan), device_id_type=pl.DeviceIdType.MESH,
+        )
+
+    w_copy = pltpu.make_async_copy(w_hbm, w_ref, w_sem)
+    w_copy.start()
+
+    barrier = pltpu.get_barrier_semaphore()
+    for o in range(1, n_seq):
+        pl.semaphore_signal(
+            barrier, inc=1, device_id=(lax.rem(s + o, n_seq), c),
+            device_id_type=pl.DeviceIdType.MESH,
+        )
+    for o in range(1, n_chan):
+        pl.semaphore_signal(
+            barrier, inc=1, device_id=(s, lax.rem(c + o, n_chan)),
+            device_id_type=pl.DeviceIdType.MESH,
+        )
+    kv_ref[...] = (k_ref[...].astype(F32) * v_ref[...].astype(F32)).astype(BF16)
+    cots_ref[c] = cot_ref[...]
+    pl.semaphore_wait(barrier, n_seq + n_chan - 2)
+
+    def rim(index, src, dst, to):
+        return remote(src, dst, rim_send.at[index], rim_recv.at[index], to, c)
+
+    @pl.when(s < n_seq - 1)
+    def _():
+        rim(0, kv_ref, prev_ref, s + 1).start()
+
+    def cot_copy(o):
+        return remote(
+            cot_ref, cots_ref.at[c], cot_send.at[o], cot_recv.at[o], s, lax.rem(c + o, n_chan)
+        )
+
+    for o in range(1, n_chan):
+        cot_copy(o).start()
+
+    @pl.when(s == 0)
+    def _():
+        prev_ref[...] = jnp.zeros_like(prev_ref)
+
+    @pl.when(s == n_seq - 1)
+    def _():
+        next_ref[...] = jnp.zeros_like(next_ref)
+
+    @pl.when(s > 0)
+    def _():
+        rim(0, kv_ref, prev_ref, s).wait_recv()
+
+    own_rows = pl.ds(pl.multiple_of(s * rows, rows), rows)
+
+    @pl.loop(0, tiles)
+    def _(tile):
+        cols = pl.ds(pl.multiple_of(tile * LANES, LANES), LANES)
+        mask = fmask_ref[...].astype(F32)
+        taps = fore_ref[pl.ds(pl.multiple_of(tile * per_tile, per_tile), per_tile), :]
+        ext = jnp.concatenate([prev_ref[:, cols], kv_ref[:, cols]], axis=0)
+        acc = jnp.zeros((rows, LANES), F32)
+        for g in range(per_tile):
+            band = (toeplitz(taps[g : g + 1, :], rows) * mask).astype(BF16)
+            res = jnp.dot(band, ext, preferred_element_type=F32)
+            acc = jnp.where(group_lanes(rows, per_group, g), res, acc)
+        filt_ref[:, cols] = acc
+        gall_ref[own_rows, cols] = (q_ref[:, cols].astype(F32) * acc).astype(BF16)
+
+    def line(side, h, seq):
+        rows_of = pl.ds(pl.multiple_of(seq * rows, rows), rows)
+        to = s + 2 if side == 0 else s - 2
+        return remote(
+            gall_ref.at[rows_of, :], gall_ref.at[rows_of, :],
+            line_send.at[side, h], line_recv.at[side, h], to, c,
+        )
+
+    def across(side, h, seq):
+        rows_of = pl.ds(pl.multiple_of(seq * rows, rows), rows)
+        return remote(
+            gall_ref.at[rows_of, :], gall_ref.at[rows_of, :],
+            pair_send.at[side, h], pair_recv.at[side, h], pair, c,
+        )
+
+    def pass_on(h):
+        up, down = s - 2 * h, s + 2 * h
+        if h > 0:
+            @pl.when(z - h >= 0)
+            def _():
+                line(0, h - 1, up).wait_recv()
+
+        @pl.when((z - h >= 0) & (z < hops - 1))
+        def _():
+            line(0, h, up).start()
+
+        @pl.when(z - h >= 0)
+        def _():
+            across(0, h, up).start()
+
+        if h > 0:
+            @pl.when(z + h < hops)
+            def _():
+                line(1, h - 1, down).wait_recv()
+
+        @pl.when((z + h < hops) & (z > 0))
+        def _():
+            line(1, h, down).start()
+
+        if h > 0:
+            @pl.when(z + h < hops)
+            def _():
+                across(1, h, down).start()
+
+    pass_on(0)
+
+    w_copy.wait()
+    for o in range(1, n_chan):
+        cot_copy(o).wait_recv()
+
+    def a2a_copy(o):
+        to = lax.rem(s + o, n_seq)
+        half_rows = pl.ds(pl.multiple_of(core * half, half), half)
+        src = cots_ref.at[
+            to // per_chan, half_rows, pl.ds(pl.multiple_of((to % per_chan) * block, block), block)
+        ]
+        dst = cotc_ref.at[pl.ds(pl.multiple_of(s * rows + core * half, half), half), :]
+        return remote(src, dst, a2a_send.at[o], a2a_recv.at[o], to, c)
+
+    for o in range(1, n_seq):
+        a2a_copy(o).start()
+
+    in_tile = 2 * LANES
+
+    @pl.loop(0, width // in_tile)
+    def _(tile):
+        cols = pl.ds(pl.multiple_of(tile * in_tile, in_tile), in_tile)
+        acc = jnp.zeros((rows, in_tile), F32)
+        for p in range(n_chan):
+            acc = acc + lax.dot_general(
+                cots_ref[p], w_ref[cols, p * width : (p + 1) * width],
+                (((1,), (1,)), ((), ())), preferred_element_type=F32,
+            )
+        gin_ref[:, cols] = acc
+        gate_ref[:, cols] = (acc * q_ref[:, cols].astype(F32)).astype(BF16)
+
+    @pl.when(s > 0)
+    def _():
+        rim(1, gate_ref, next_ref, s - 1).start()
+
+    cotc_ref[own_rows, :] = cots_ref[
+        s // per_chan, :, pl.ds(pl.multiple_of((s % per_chan) * block, block), block)
+    ]
+    pass_on(1)
+
+    def part_copy(o):
+        to = lax.rem(c + o, n_chan)
+        return remote(
+            psend_ref.at[to], precv_ref.at[c], part_send.at[o], part_recv.at[o], s, to
+        )
+
+    gated = gall_ref.at[own_rows, :]
+    for o in range(1, n_chan + 1):
+        to = lax.rem(c + o, n_chan)
+        dest = psend_ref if o < n_chan else precv_ref
+
+        @pl.loop(0, width // in_tile)
+        def _(tile):
+            cols = pl.ds(pl.multiple_of(tile * in_tile, in_tile), in_tile)
+            w_cols = pl.ds(pl.multiple_of(to * width + tile * in_tile, in_tile), in_tile)
+            dest[to, :, cols] = jnp.dot(
+                gated[...], w_ref[:, w_cols], preferred_element_type=F32
+            ).astype(BF16)
+
+        if o < n_chan:
+            part_copy(o).start()
+
+    for h in range(2, hops - 1):
+        pass_on(h)
+
+    def share_copy(o):
+        came = lax.rem(s + n_seq - o, n_seq)
+        at = pl.ds(pl.multiple_of(came * rows + core * half, half), half)
+        return remote(
+            cotc_ref.at[at, :], cotc_ref.at[at, :], share_send.at[o], share_recv.at[o], s, mate
+        )
+
+    @pl.when(s < n_seq - 1)
+    def _():
+        rim(1, gate_ref, next_ref, s).wait_recv()
+
+    r = lax.broadcasted_iota(jnp.int32, (rows, rows), 0)
+    cc = lax.broadcasted_iota(jnp.int32, (rows, rows), 1)
+    turn = jnp.where(r + cc == rows - 1, 1.0, 0.0).astype(BF16)
+
+    @pl.loop(0, tiles)
+    def _(tile):
+        cols = pl.ds(pl.multiple_of(tile * LANES, LANES), LANES)
+        at = pl.ds(pl.multiple_of(tile * per_tile, per_tile), per_tile)
+        bmask = bmask_ref[...].astype(F32)
+        rmask = rmask_ref[...].astype(F32)
+        taps = back_ref[at, :]
+        gate = gate_ref[:, cols]
+        gext = jnp.concatenate([gate, next_ref[:, cols]], axis=0)
+        ext = jnp.concatenate([prev_ref[:, cols], kv_ref[:, cols]], axis=0)
+        turned = jnp.dot(turn, gate, preferred_element_type=F32)
+        acc = jnp.zeros((rows, LANES), F32)
+        found = []
+        for g in range(per_tile):
+            lanes = group_lanes(rows, per_group, g)
+            band = (toeplitz(taps[g : g + 1, :], rows) * bmask).astype(BF16)
+            res = jnp.dot(band, gext, preferred_element_type=F32)
+            acc = jnp.where(lanes, res, acc)
+            mine = jnp.where(lanes, turned, 0.0).astype(BF16)
+            terms = lax.dot_general(
+                mine, ext, (((1,), (1,)), ((), ())), preferred_element_type=F32
+            )
+            terms = pltpu.roll(terms * rmask, 0, 1, stride=1, stride_axis=0)
+            found.append(jnp.sum(terms, axis=0, keepdims=True))
+        sums_ref[at, :] = jnp.concatenate(found, axis=0)
+        gq_ref[:, cols] = (gin_ref[:, cols] * filt_ref[:, cols]).astype(BF16)
+        gk_ref[:, cols] = (acc * v_ref[:, cols].astype(F32)).astype(BF16)
+        gv_ref[:, cols] = (acc * k_ref[:, cols].astype(F32)).astype(BF16)
+
+    tsend_ref[...] = sums_ref[:, sums_ref.shape[1] - LANES :].astype(BF16)
+
+    def tap_copy(o):
+        return remote(
+            tsend_ref, trecv_ref.at[s], tap_send.at[o], tap_recv.at[o], lax.rem(s + o, n_seq), c
+        )
+
+    for o in range(1, n_seq):
+        tap_copy(o).start()
+    trecv_ref[s] = tsend_ref[...]
+
+    for o in range(1, n_seq):
+        a2a_copy(o).wait_recv()
+        share_copy(o).start()
+    for h in range(max(2, hops - 1), hops):
+        pass_on(h)
+
+    for o in range(1, n_chan):
+        part_copy(o).wait_recv()
+
+    @pl.loop(0, width // in_tile)
+    def _(tile):
+        cols = pl.ds(pl.multiple_of(tile * in_tile, in_tile), in_tile)
+        acc = precv_ref[0, :, cols].astype(F32)
+        for p in range(1, n_chan):
+            acc = acc + precv_ref[p, :, cols].astype(F32)
+        out_ref[:, cols] = acc.astype(BF16)
+
+    for o in range(1, n_seq):
+        tap_copy(o).wait_recv()
+    total = trecv_ref[0].astype(F32)
+    for p in range(1, n_seq):
+        total = total + trecv_ref[p].astype(F32)
+    tap_ref[...] = total
+
+    for o in range(1, n_seq):
+        share_copy(o).wait_recv()
+    for h in range(hops):
+        @pl.when(z - h >= 0)
+        def _():
+            across(0, h, s - 2 * h).wait_recv()
+
+        if h > 0:
+            @pl.when(z + h < hops)
+            def _():
+                across(1, h, s + 2 * h).wait_recv()
+
+    @pl.loop(0, width // in_tile)
+    def _(tile):
+        cols = pl.ds(pl.multiple_of(tile * in_tile, in_tile), in_tile)
+        gw_ref[cols, :] = lax.dot_general(
+            gall_ref[:, cols], cotc_ref[...], (((0,), (0,)), ((), ())),
+            preferred_element_type=F32,
+        ).astype(BF16)
+
+    @pl.when(s < n_seq - 1)
+    def _():
+        rim(0, kv_ref, prev_ref, s + 1).wait_send()
+
+    @pl.when(s > 0)
+    def _():
+        rim(1, gate_ref, next_ref, s - 1).wait_send()
+
+    for o in range(1, n_chan):
+        cot_copy(o).wait_send()
+        part_copy(o).wait_send()
+    for o in range(1, n_seq):
+        a2a_copy(o).wait_send()
+        share_copy(o).wait_send()
+        tap_copy(o).wait_send()
+    for h in range(hops):
+        @pl.when((z - h >= 0) & (z < hops - 1))
+        def _():
+            line(0, h, s - 2 * h).wait_send()
+
+        @pl.when((z + h < hops) & (z > 0))
+        def _():
+            line(1, h, s + 2 * h).wait_send()
+
+        @pl.when(z - h >= 0)
+        def _():
+            across(0, h, s - 2 * h).wait_send()
+
+        if h > 0:
+            @pl.when(z + h < hops)
+            def _():
+                across(1, h, s + 2 * h).wait_send()
+
+
+def fused_body(n_seq, n_chan, query_in, key_in, value_in, filters, doc_lengths, w_out, cotangent):
+    rows, width = query_in.shape
+    groups, length = filters.shape
+    per_group = width // groups
+    block = w_out.shape[1] // n_seq
+    fore_taps, back_taps, fmask, bmask = prepare(rows, filters, doc_lengths)
+    vmem = pl.BlockSpec(memory_space=pltpu.VMEM)
+    act = jax.ShapeDtypeStruct((rows, width), BF16)
+    dma = pltpu.SemaphoreType.DMA
+    hops = n_seq // 2
+    block_out, grad_query, grad_key, grad_value, weight, taps = pl.pallas_call(
+        functools.partial(mega_kernel, per_group, n_seq, n_chan),
+        in_specs=[vmem] * 9 + [pl.BlockSpec(memory_space=pl.ANY)],
+        out_specs=[vmem] * 6,
+        out_shape=[act] * 4
+        + [
+            jax.ShapeDtypeStruct((width, block), BF16),
+            jax.ShapeDtypeStruct((groups, length), F32),
+        ],
+        scratch_shapes=[
+            pltpu.VMEM(w_out.shape, BF16),
+            pltpu.VMEM((rows, width), BF16),
+            pltpu.VMEM((rows, width), BF16),
+            pltpu.VMEM((rows, width), BF16),
+            pltpu.VMEM((rows, width), BF16),
+            pltpu.VMEM((rows, width), F32),
+            pltpu.VMEM((rows, width), F32),
+            pltpu.VMEM((n_seq * rows, width), BF16),
+            pltpu.VMEM((n_chan, rows, width), BF16),
+            pltpu.VMEM((n_seq * rows, block), BF16),
+            pltpu.VMEM((n_chan, rows, width), BF16),
+            pltpu.VMEM((n_chan, rows, width), BF16),
+            pltpu.VMEM((groups, length), BF16),
+            pltpu.VMEM((n_seq, groups, length), BF16),
+            pltpu.VMEM((groups, 2 * rows), F32),
+            dma, dma((2,)), dma((2,)), dma((n_chan,)), dma((n_chan,)), dma((n_chan,)),
+            dma((n_chan,)), dma((n_seq,)), dma((n_seq,)), dma((n_seq,)), dma((n_seq,)),
+            dma((n_seq,)), dma((n_seq,)), dma((2, hops)), dma((2, hops)), dma((2, hops)),
+            dma((2, hops)),
+        ],
+        compiler_params=pltpu.CompilerParams(
+            collective_id=0, has_side_effects=True, vmem_limit_bytes=56 * 2**20
+        ),
+    )(
+        query_in, key_in, value_in, cotangent, fore_taps, back_taps, fmask, jnp.flip(fmask, 0),
+        bmask, w_out,
+    )
+    share = length // n_seq
+    at = length - (lax.axis_index("seq") + 1) * share
+    tap_sum = jnp.flip(lax.dynamic_slice_in_dim(taps, at, share, axis=1), 1)
+    return (block_out, grad_query, grad_key, grad_value, weight, tap_sum)
+
+
+def program(n_seq, n_chan, *arrays):
+    rows, width = arrays[0].shape
+    groups, length = arrays[3].shape
+    block = arrays[5].shape[1] // n_seq
+    aligned = block % LANES == 0 and width % block == 0 and width % (2 * LANES) == 0
+    even = n_seq % 2 == 0 and n_chan % 2 == 0 and n_seq >= 4
+    if aligned and even and rows == length == LANES and LANES * groups % width == 0:
+        return fused_body(n_seq, n_chan, *arrays)
+    return body(n_seq, *arrays)
+
+
 def solution(mesh):
     act = P("seq", "chan")
     return jax.shard_map(
-        functools.partial(body, mesh.shape["seq"]),
+        functools.partial(program, mesh.shape["seq"], mesh.shape["chan"]),
         mesh=mesh,
         in_specs=(act, act, act, P("chan", None), P(), P("chan", None), act),
         out_specs=(act, act, act, act, P("chan", "seq"), P("chan", "seq")),

time: 239 us -> 106 us (0.44)
  the two profiles are of different devices: /device:TPU:0 before, /device:TPU:4 now
where the time goes in v2:
time: 106 us; the launch traced here: 105 us
  Pallas kernels  89.4 us (84%)
  local copies, waits for them, and re-layouts  12.6 us (12%)
  other arithmetic  2.46 us (2%)
    pallas_call x1, Pallas kernels, fused_body(): pl.pallas_call(functools.partial(mega_kernel, per_group, n_seq, n_chan),...  89.4 us
    unnamed x14, local copies, waits for them, and re-layouts  9.44 us

profile of v2, /device:TPU:4, one launch (start us, length us, event | category | flops | bytes accessed | tf_op | source)
XLA Modules:
  0.0 105.2 jit_solution(15291843565114846532)
XLA Ops:
  0.7 0.7 copy.17
  1.5 0.1 reduce
  1.6 0.7 sub.10
  2.2 0.1 select_reduce_fusion
  2.3 0.1 select_reduce_fusion.1
  2.4 0.7 pad_convert_fusion.back_ref
  3.2 0.0 copy-start.1
  3.2 0.2 reverse.2
  3.3 0.1 slice.18
  3.4 0.7 concatenate.11.fore_ref
  4.1 0.7 compare_convert_fusion
  4.8 0.0 copy-start.2
  4.8 0.7 rev.10.rmask_ref
  5.5 0.0 copy-done.1
  5.5 0.0 copy-done.2
  5.5 89.4 %shard_map.118 = (bf16[128,1536]{1,0:T(8,128)(2,1)}, bf16[128,1536]{1,0:T(8,128)(2,1)}, bf16[128,1536]{1,0:T(8,128)(2,1)}, bf16[128,1536]{1,0:T(8,128)(2,1)}, bf...) custom-call(bf16[128,1536]{1,0:T(8,128)(2,1)} %q_ref.1, bf16[128,1536]{1,0:T(8,128)(2,1)} %k_ref.1, bf16[128,1536]{1,0:T(8,128)(2,1)} %v_ref.1, ...), custom_call_target="tpu_custom_call" | custom-call | tf_op jit(solution)/shard_map/pallas_call | solution.py:505
  94.9 0.0 copy-start
  94.9 1.0 constant_dynamic-slice_fusion
  95.9 0.1 rev.11
  96.0 0.7 copy.18
  96.7 1.8 %copy.24 = bf16[128,1536]{1,0:T(8,128)(2,1)} copy(bf16[128,1536]{1,0:T(8,128)(2,1)} %get-tuple-element.44) | data formatting | bytes 786432
  98.5 1.8 %copy.25 = bf16[128,1536]{1,0:T(8,128)(2,1)} copy(bf16[128,1536]{1,0:T(8,128)(2,1)} %get-tuple-element.45) | data formatting | bytes 786432
  100.2 1.8 %copy.26 = bf16[128,1536]{1,0:T(8,128)(2,1)} copy(bf16[128,1536]{1,0:T(8,128)(2,1)} %get-tuple-element.46) | data formatting | bytes 786432
  102.0 1.8 %copy.27 = bf16[128,1536]{1,0:T(8,128)(2,1)} copy(bf16[128,1536]{1,0:T(8,128)(2,1)} %get-tuple-element.47) | data formatting | bytes 786432
  103.8 0.0 copy-done
  103.8 1.4 %copy.28 = bf16[1536,768]{1,0:T(8,128)(2,1)} copy(bf16[1536,768]{1,0:T(8,128)(2,1)S(1)} %copy-done) | data formatting | bytes 4718592
  (5 shorter events, 0.1 us)
Async XLA Ops:
  3.2 2.3 %copy-start.1 = (f32[96,256]{1,0:T(8,128)}, f32[96,256]{1,0:T(8,128)S(1)}, u32[]{:S(2)}) copy-start(f32[96,256]{1,0:T(8,128)S(1)} %pad_convert_fusion.back_ref) | copy-start | bytes 294916
  4.8 0.7 copy-start.2
  94.9 8.9 %copy-start = (bf16[1536,768]{1,0:T(8,128)(2,1)S(1)}, bf16[1536,768]{1,0:T(8,128)(2,1)}, u32[]{:S(2)}) copy-start(bf16[1536,768]{1,0:T(8,128)(2,1)} %get-tuple-element.48) | copy-start | bytes 7077892

commit v3 on v2

--- a/solution.py
+++ b/solution.py
@@ -17,9 +17,9 @@
     return jnp.max(jnp.where(before, starts[None, :], 0), axis=1)
 
 
-def toeplitz(row, rows):
+def toeplitz(row, rows, shift=0):
     wide = jnp.broadcast_to(row, (rows, row.shape[-1]))
-    return pltpu.roll(wide, 0, 1, stride=1, stride_axis=0)
+    return pltpu.roll(wide, shift, 1, stride=1, stride_axis=0)
 
 
 def group_lanes(rows, per_group, index):
@@ -161,19 +161,22 @@
 
 
 def mega_kernel(
-    per_group, n_seq, n_chan, q_ref, k_ref, v_ref, cot_ref, fore_ref, back_ref, fmask_ref, rmask_ref,
-    bmask_ref, w_hbm, out_ref, gq_ref, gk_ref, gv_ref, gw_ref, tap_ref,
+    per_group, n_seq, n_chan, chunks, q_ref, k_ref, v_ref, cot_ref, taps_ref, len_ref, w_hbm,
+    out_ref, gq_ref, gk_ref, gv_ref, gw_ref, tap_ref,
     w_ref, kv_ref, prev_ref, gate_ref, next_ref, filt_ref, gin_ref, gall_ref, cots_ref, cotc_ref,
-    psend_ref, precv_ref, tsend_ref, trecv_ref, sums_ref,
-    w_sem, rim_send, rim_recv, cot_send, cot_recv, part_send, part_recv, a2a_send, a2a_recv,
-    share_send, share_recv, tap_send, tap_recv, line_send, line_recv, pair_send, pair_recv,
+    psend_ref, precv_ref, tsend_ref, trecv_ref, sums_ref, fore_ref, back_ref, fmask_ref, rmask_ref, bmask_ref,
+    w_sem, rim_send, rim_recv, cot_send, cot_recv, pass_send, pass_recv, part_send, part_recv,
+    a2a_send, a2a_recv, share_send, share_recv, tap_send, tap_recv, line_send, line_recv,
+    pair_send, pair_recv,
 ):
     rows, width = q_ref.shape
+    span = 2 * rows
     block = gw_ref.shape[1]
     per_chan = width // block
     half = rows // 2
-    tiles = width // LANES
     per_tile = LANES // per_group
+    piece = width // chunks
+    piece_tiles = piece // LANES
     s = lax.axis_index("seq")
     c = lax.axis_index("chan")
     hops = n_seq // 2
@@ -204,22 +207,27 @@
         )
     kv_ref[...] = (k_ref[...].astype(F32) * v_ref[...].astype(F32)).astype(BF16)
     cots_ref[c] = cot_ref[...]
-    pl.semaphore_wait(barrier, n_seq + n_chan - 2)
-
-    def rim(index, src, dst, to):
-        return remote(src, dst, rim_send.at[index], rim_recv.at[index], to, c)
-
-    @pl.when(s < n_seq - 1)
-    def _():
-        rim(0, kv_ref, prev_ref, s + 1).start()
-
-    def cot_copy(o):
-        return remote(
-            cot_ref, cots_ref.at[c], cot_send.at[o], cot_recv.at[o], s, lax.rem(c + o, n_chan)
-        )
-
-    for o in range(1, n_chan):
-        cot_copy(o).start()
+
+    row = lax.broadcasted_iota(jnp.int32, (rows, span), 0) + s * rows
+    lane = lax.broadcasted_iota(jnp.int32, (rows, span), 1) + s * rows
+    turned_row = 2 * s * rows + rows - 1 - row
+
+    def first(pos):
+        best = jnp.zeros_like(pos)
+        start = jnp.int32(0)
+        for d in range(len_ref.shape[0]):
+            best = jnp.where(start <= pos, start, best)
+            start = start + len_ref[d]
+        return best
+
+    fmask_ref[...] = jnp.where(lane - rows >= first(row), 1.0, 0.0)
+    rmask_ref[...] = jnp.where(lane - rows >= first(turned_row), 1.0, 0.0)
+    bmask_ref[...] = jnp.where(row >= first(lane), 1.0, 0.0)
+    r = lax.broadcasted_iota(jnp.int32, (rows, rows), 0)
+    cc = lax.broadcasted_iota(jnp.int32, (rows, rows), 1)
+    turn = jnp.where(r + cc == rows - 1, 1.0, 0.0).astype(BF16)
+    back_ref[...] = taps_ref[...].astype(F32)
+    fore_ref[...] = jnp.dot(taps_ref[...], turn, preferred_element_type=F32)
 
     @pl.when(s == 0)
     def _():
@@ -229,75 +237,105 @@
     def _():
         next_ref[...] = jnp.zeros_like(next_ref)
 
-    @pl.when(s > 0)
+    pl.semaphore_wait(barrier, n_seq + n_chan - 2)
+
+    def rim(index, src, dst, ch, to):
+        cols = pl.ds(ch * piece, piece)
+        return remote(
+            src.at[:, cols], dst.at[:, cols], rim_send.at[index, ch], rim_recv.at[index, ch], to, c
+        )
+
+    @pl.when(s < n_seq - 1)
     def _():
-        rim(0, kv_ref, prev_ref, s).wait_recv()
+        for ch in range(chunks):
+            rim(0, kv_ref, prev_ref, ch, s + 1).start()
+
+    def cot_copy(o):
+        to = mate if o == 0 else lax.rem(c + 2 * o, n_chan)
+        return remote(cot_ref, cots_ref.at[c], cot_send.at[o], cot_recv.at[o], s, to)
+
+    def cot_pass(o):
+        came = lax.rem(c + n_chan - 2 * o, n_chan)
+        return remote(
+            cots_ref.at[came], cots_ref.at[came], pass_send.at[o], pass_recv.at[o], s, mate
+        )
+
+    chips = n_chan // 2
+    for o in range(1, chips):
+        cot_copy(o).start()
+    cot_copy(0).start()
 
     own_rows = pl.ds(pl.multiple_of(s * rows, rows), rows)
 
-    @pl.loop(0, tiles)
-    def _(tile):
-        cols = pl.ds(pl.multiple_of(tile * LANES, LANES), LANES)
-        mask = fmask_ref[...].astype(F32)
-        taps = fore_ref[pl.ds(pl.multiple_of(tile * per_tile, per_tile), per_tile), :]
-        ext = jnp.concatenate([prev_ref[:, cols], kv_ref[:, cols]], axis=0)
-        acc = jnp.zeros((rows, LANES), F32)
-        for g in range(per_tile):
-            band = (toeplitz(taps[g : g + 1, :], rows) * mask).astype(BF16)
-            res = jnp.dot(band, ext, preferred_element_type=F32)
-            acc = jnp.where(group_lanes(rows, per_group, g), res, acc)
-        filt_ref[:, cols] = acc
-        gall_ref[own_rows, cols] = (q_ref[:, cols].astype(F32) * acc).astype(BF16)
-
-    def line(side, h, seq):
+    def line(side, h, ch, seq):
         rows_of = pl.ds(pl.multiple_of(seq * rows, rows), rows)
+        part = gall_ref.at[rows_of, pl.ds(ch * piece, piece)]
         to = s + 2 if side == 0 else s - 2
-        return remote(
-            gall_ref.at[rows_of, :], gall_ref.at[rows_of, :],
-            line_send.at[side, h], line_recv.at[side, h], to, c,
-        )
-
-    def across(side, h, seq):
+        return remote(part, part, line_send.at[side, h, ch], line_recv.at[side, h, ch], to, c)
+
+    def across(side, h, ch, seq):
         rows_of = pl.ds(pl.multiple_of(seq * rows, rows), rows)
-        return remote(
-            gall_ref.at[rows_of, :], gall_ref.at[rows_of, :],
-            pair_send.at[side, h], pair_recv.at[side, h], pair, c,
-        )
-
-    def pass_on(h):
+        part = gall_ref.at[rows_of, pl.ds(ch * piece, piece)]
+        return remote(part, part, pair_send.at[side, h, ch], pair_recv.at[side, h, ch], pair, c)
+
+    def pass_on(h, ch):
         up, down = s - 2 * h, s + 2 * h
         if h > 0:
             @pl.when(z - h >= 0)
             def _():
-                line(0, h - 1, up).wait_recv()
+                line(0, h - 1, ch, up).wait_recv()
 
         @pl.when((z - h >= 0) & (z < hops - 1))
         def _():
-            line(0, h, up).start()
+            line(0, h, ch, up).start()
 
         @pl.when(z - h >= 0)
         def _():
-            across(0, h, up).start()
+            across(0, h, ch, up).start()
 
         if h > 0:
             @pl.when(z + h < hops)
             def _():
-                line(1, h - 1, down).wait_recv()
+                line(1, h - 1, ch, down).wait_recv()
 
         @pl.when((z + h < hops) & (z > 0))
         def _():
-            line(1, h, down).start()
+            line(1, h, ch, down).start()
 
         if h > 0:
             @pl.when(z + h < hops)
             def _():
-                across(1, h, down).start()
-
-    pass_on(0)
-
+                across(1, h, ch, down).start()
+
+    for ch in range(chunks):
+        @pl.when(s > 0)
+        def _():
+            rim(0, kv_ref, prev_ref, ch, s).wait_recv()
+
+        @pl.loop(ch * piece_tiles, (ch + 1) * piece_tiles)
+        def _(tile):
+            cols = pl.ds(pl.multiple_of(tile * LANES, LANES), LANES)
+            mask = fmask_ref[...]
+            taps = fore_ref[pl.ds(pl.multiple_of(tile * per_tile, per_tile), per_tile), :]
+            taps = jnp.concatenate([taps, jnp.zeros_like(taps)], axis=1)
+            ext = jnp.concatenate([prev_ref[:, cols], kv_ref[:, cols]], axis=0)
+            acc = jnp.zeros((rows, LANES), F32)
+            for g in range(per_tile):
+                band = (toeplitz(taps[g : g + 1, :], rows, 1) * mask).astype(BF16)
+                res = jnp.dot(band, ext, preferred_element_type=F32)
+                acc = jnp.where(group_lanes(rows, per_group, g), res, acc)
+            filt_ref[:, cols] = acc
+            gall_ref[own_rows, cols] = (q_ref[:, cols].astype(F32) * acc).astype(BF16)
+
+        pass_on(0, ch)
+
+    for o in range(1, chips):
+        cot_copy(o).wait_recv()
+        cot_pass(o).start()
+    cot_copy(0).wait_recv()
     w_copy.wait()
-    for o in range(1, n_chan):
-        cot_copy(o).wait_recv()
+    for o in range(1, chips):
+        cot_pass(o).wait_recv()
 
     def a2a_copy(o):
         to = lax.rem(s + o, n_seq)
@@ -312,27 +350,30 @@
         a2a_copy(o).start()
 
     in_tile = 2 * LANES
-
-    @pl.loop(0, width // in_tile)
-    def _(tile):
-        cols = pl.ds(pl.multiple_of(tile * in_tile, in_tile), in_tile)
-        acc = jnp.zeros((rows, in_tile), F32)
-        for p in range(n_chan):
-            acc = acc + lax.dot_general(
-                cots_ref[p], w_ref[cols, p * width : (p + 1) * width],
-                (((1,), (1,)), ((), ())), preferred_element_type=F32,
-            )
-        gin_ref[:, cols] = acc
-        gate_ref[:, cols] = (acc * q_ref[:, cols].astype(F32)).astype(BF16)
-
-    @pl.when(s > 0)
-    def _():
-        rim(1, gate_ref, next_ref, s - 1).start()
+    piece_ins = piece // in_tile
+
+    for ch in range(chunks):
+        @pl.loop(ch * piece_ins, (ch + 1) * piece_ins)
+        def _(tile):
+            cols = pl.ds(pl.multiple_of(tile * in_tile, in_tile), in_tile)
+            acc = jnp.zeros((rows, in_tile), F32)
+            for p in range(n_chan):
+                acc = acc + lax.dot_general(
+                    cots_ref[p], w_ref[cols, p * width : (p + 1) * width],
+                    (((1,), (1,)), ((), ())), preferred_element_type=F32,
+                )
+            gin_ref[:, cols] = acc
+            gate_ref[:, cols] = (acc * q_ref[:, cols].astype(F32)).astype(BF16)
+
+        @pl.when(s > 0)
+        def _():
+            rim(1, gate_ref, next_ref, ch, s - 1).start()
+
+        pass_on(1, ch)
 
     cotc_ref[own_rows, :] = cots_ref[
         s // per_chan, :, pl.ds(pl.multiple_of((s % per_chan) * block, block), block)
     ]
-    pass_on(1)
 
     def part_copy(o):
         to = lax.rem(c + o, n_chan)
@@ -341,6 +382,8 @@
         )
 
     gated = gall_ref.at[own_rows, :]
+    later = [(h, ch) for h in range(2, hops) for ch in range(chunks)]
+    waiting = later[:chunks]
     for o in range(1, n_chan + 1):
         to = lax.rem(c + o, n_chan)
         dest = psend_ref if o < n_chan else precv_ref
@@ -355,9 +398,10 @@
 
         if o < n_chan:
             part_copy(o).start()
-
-    for h in range(2, hops - 1):
-        pass_on(h)
+        if waiting:
+            pass_on(*waiting.pop(0))
+    for left in waiting:
+        pass_on(*left)
 
     def share_copy(o):
         came = lax.rem(s + n_seq - o, n_seq)
@@ -366,44 +410,50 @@
             cotc_ref.at[at, :], cotc_ref.at[at, :], share_send.at[o], share_recv.at[o], s, mate
         )
 
-    @pl.when(s < n_seq - 1)
-    def _():
-        rim(1, gate_ref, next_ref, s).wait_recv()
-
-    r = lax.broadcasted_iota(jnp.int32, (rows, rows), 0)
-    cc = lax.broadcasted_iota(jnp.int32, (rows, rows), 1)
-    turn = jnp.where(r + cc == rows - 1, 1.0, 0.0).astype(BF16)
-
-    @pl.loop(0, tiles)
-    def _(tile):
-        cols = pl.ds(pl.multiple_of(tile * LANES, LANES), LANES)
-        at = pl.ds(pl.multiple_of(tile * per_tile, per_tile), per_tile)
-        bmask = bmask_ref[...].astype(F32)
-        rmask = rmask_ref[...].astype(F32)
-        taps = back_ref[at, :]
-        gate = gate_ref[:, cols]
-        gext = jnp.concatenate([gate, next_ref[:, cols]], axis=0)
-        ext = jnp.concatenate([prev_ref[:, cols], kv_ref[:, cols]], axis=0)
-        turned = jnp.dot(turn, gate, preferred_element_type=F32)
-        acc = jnp.zeros((rows, LANES), F32)
-        found = []
-        for g in range(per_tile):
-            lanes = group_lanes(rows, per_group, g)
-            band = (toeplitz(taps[g : g + 1, :], rows) * bmask).astype(BF16)
-            res = jnp.dot(band, gext, preferred_element_type=F32)
-            acc = jnp.where(lanes, res, acc)
-            mine = jnp.where(lanes, turned, 0.0).astype(BF16)
-            terms = lax.dot_general(
-                mine, ext, (((1,), (1,)), ((), ())), preferred_element_type=F32
-            )
-            terms = pltpu.roll(terms * rmask, 0, 1, stride=1, stride_axis=0)
-            found.append(jnp.sum(terms, axis=0, keepdims=True))
-        sums_ref[at, :] = jnp.concatenate(found, axis=0)
-        gq_ref[:, cols] = (gin_ref[:, cols] * filt_ref[:, cols]).astype(BF16)
-        gk_ref[:, cols] = (acc * v_ref[:, cols].astype(F32)).astype(BF16)
-        gv_ref[:, cols] = (acc * k_ref[:, cols].astype(F32)).astype(BF16)
-
-    tsend_ref[...] = sums_ref[:, sums_ref.shape[1] - LANES :].astype(BF16)
+    waiting = later[chunks:]
+    for ch in range(chunks):
+        @pl.when(s < n_seq - 1)
+        def _():
+            rim(1, gate_ref, next_ref, ch, s).wait_recv()
+
+        @pl.loop(ch * piece_tiles, (ch + 1) * piece_tiles)
+        def _(tile):
+            cols = pl.ds(pl.multiple_of(tile * LANES, LANES), LANES)
+            at = pl.ds(pl.multiple_of(tile * per_tile, per_tile), per_tile)
+            bmask = bmask_ref[...]
+            rmask = rmask_ref[...]
+            taps = back_ref[at, :]
+            taps = jnp.concatenate([taps, jnp.zeros_like(taps)], axis=1)
+            gate = gate_ref[:, cols]
+            gext = jnp.concatenate([gate, next_ref[:, cols]], axis=0)
+            ext = jnp.concatenate([prev_ref[:, cols], kv_ref[:, cols]], axis=0)
+            turned = jnp.dot(turn, gate, preferred_element_type=F32)
+            acc = jnp.zeros((rows, LANES), F32)
+            found = []
+            for g in range(per_tile):
+                lanes = group_lanes(rows, per_group, g)
+                band = (toeplitz(taps[g : g + 1, :], rows) * bmask).astype(BF16)
+                res = jnp.dot(band, gext, preferred_element_type=F32)
+                acc = jnp.where(lanes, res, acc)
+                mine = jnp.where(lanes, turned, 0.0).astype(BF16)
+                terms = lax.dot_general(
+                    mine, ext, (((1,), (1,)), ((), ())), preferred_element_type=F32
+                )
+                terms = pltpu.roll(terms * rmask, 0, 1, stride=1, stride_axis=0)
+                found.append(jnp.sum(terms, axis=0, keepdims=True))
+            sums_ref[at, :] = jnp.concatenate(found, axis=0)
+            gq_ref[:, cols] = (gin_ref[:, cols] * filt_ref[:, cols]).astype(BF16)
+            gk_ref[:, cols] = (acc * v_ref[:, cols].astype(F32)).astype(BF16)
+            gv_ref[:, cols] = (acc * k_ref[:, cols].astype(F32)).astype(BF16)
+
+        if waiting:
+            pass_on(*waiting.pop(0))
+    for left in waiting:
+        pass_on(*left)
+
+    tsend_ref[...] = jnp.dot(
+        sums_ref[:, span - LANES :].astype(BF16), turn, preferred_element_type=F32
+    ).astype(BF16)
 
     def tap_copy(o):
         return remote(
@@ -417,8 +467,6 @@
     for o in range(1, n_seq):
         a2a_copy(o).wait_recv()
         share_copy(o).start()
-    for h in range(max(2, hops - 1), hops):
-        pass_on(h)
 
     for o in range(1, n_chan):
         part_copy(o).wait_recv()
@@ -436,60 +484,68 @@
     total = trecv_ref[0].astype(F32)
     for p in range(1, n_seq):
         total = total + trecv_ref[p].astype(F32)
-    tap_ref[...] = total
+    share = tap_ref.shape[1]
+    total = pltpu.roll(total, lax.rem(LANES - s * share, LANES), 1)
+    tap_ref[...] = total[:, :share]
 
     for o in range(1, n_seq):
         share_copy(o).wait_recv()
-    for h in range(hops):
-        @pl.when(z - h >= 0)
-        def _():
-            across(0, h, s - 2 * h).wait_recv()
-
-        if h > 0:
-            @pl.when(z + h < hops)
+    for ch in range(chunks):
+        for h in range(hops):
+            @pl.when(z - h >= 0)
             def _():
-                across(1, h, s + 2 * h).wait_recv()
-
-    @pl.loop(0, width // in_tile)
-    def _(tile):
-        cols = pl.ds(pl.multiple_of(tile * in_tile, in_tile), in_tile)
-        gw_ref[cols, :] = lax.dot_general(
-            gall_ref[:, cols], cotc_ref[...], (((0,), (0,)), ((), ())),
-            preferred_element_type=F32,
-        ).astype(BF16)
-
-    @pl.when(s < n_seq - 1)
-    def _():
-        rim(0, kv_ref, prev_ref, s + 1).wait_send()
-
-    @pl.when(s > 0)
-    def _():
-        rim(1, gate_ref, next_ref, s - 1).wait_send()
-
+                across(0, h, ch, s - 2 * h).wait_recv()
+
+            if h > 0:
+                @pl.when(z + h < hops)
+                def _():
+                    across(1, h, ch, s + 2 * h).wait_recv()
+
+        @pl.loop(ch * piece_ins, (ch + 1) * piece_ins)
+        def _(tile):
+            cols = pl.ds(pl.multiple_of(tile * in_tile, in_tile), in_tile)
+            gw_ref[cols, :] = lax.dot_general(
+                gall_ref[:, cols], cotc_ref[...], (((0,), (0,)), ((), ())),
+                preferred_element_type=F32,
+            ).astype(BF16)
+
+    for ch in range(chunks):
+        @pl.when(s < n_seq - 1)
+        def _():
+            rim(0, kv_ref, prev_ref, ch, s + 1).wait_send()
+
+        @pl.when(s > 0)
+        def _():
+            rim(1, gate_ref, next_ref, ch, s - 1).wait_send()
+
+    for o in range(chips):
+        cot_copy(o).wait_send()
+    for o in range(1, chips):
+        cot_pass(o).wait_send()
     for o in range(1, n_chan):
-        cot_copy(o).wait_send()
         part_copy(o).wait_send()
     for o in range(1, n_seq):
         a2a_copy(o).wait_send()
         share_copy(o).wait_send()
         tap_copy(o).wait_send()
     for h in range(hops):
-        @pl.when((z - h >= 0) & (z < hops - 1))
-        def _():
-            line(0, h, s - 2 * h).wait_send()
-
-        @pl.when((z + h < hops) & (z > 0))
-        def _():
-            line(1, h, s + 2 * h).wait_send()
-
-        @pl.when(z - h >= 0)
-        def _():
-            across(0, h, s - 2 * h).wait_send()
-
-        if h > 0:
-            @pl.when(z + h < hops)
+        for ch in range(chunks):
+            @pl.when((z - h >= 0) & (z < hops - 1))
             def _():
-                across(1, h, s + 2 * h).wait_send()
+                line(0, h, ch, s - 2 * h).wait_send()
+
+            @pl.when((z + h < hops) & (z > 0))
+            def _():
+                line(1, h, ch, s + 2 * h).wait_send()
+
+            @pl.when(z - h >= 0)
+            def _():
+                across(0, h, ch, s - 2 * h).wait_send()
+
+            if h > 0:
+                @pl.when(z + h < hops)
+                def _():
+                    across(1, h, ch, s + 2 * h).wait_send()
 
 
 def fused_body(n_seq, n_chan, query_in, key_in, value_in, filters, doc_lengths, w_out, cotangent):
@@ -497,19 +553,21 @@
     groups, length = filters.shape
     per_group = width // groups
     block = w_out.shape[1] // n_seq
-    fore_taps, back_taps, fmask, bmask = prepare(rows, filters, doc_lengths)
+    ins = width // (2 * LANES)
+    chunks = 3 if ins % 3 == 0 else 2 if ins % 2 == 0 else 1
     vmem = pl.BlockSpec(memory_space=pltpu.VMEM)
     act = jax.ShapeDtypeStruct((rows, width), BF16)
     dma = pltpu.SemaphoreType.DMA
     hops = n_seq // 2
-    block_out, grad_query, grad_key, grad_value, weight, taps = pl.pallas_call(
-        functools.partial(mega_kernel, per_group, n_seq, n_chan),
-        in_specs=[vmem] * 9 + [pl.BlockSpec(memory_space=pl.ANY)],
+    results = pl.pallas_call(
+        functools.partial(mega_kernel, per_group, n_seq, n_chan, chunks),
+        in_specs=[vmem] * 5
+        + [pl.BlockSpec(memory_space=pltpu.SMEM), pl.BlockSpec(memory_space=pl.ANY)],
         out_specs=[vmem] * 6,
         out_shape=[act] * 4
         + [
             jax.ShapeDtypeStruct((width, block), BF16),
-            jax.ShapeDtypeStruct((groups, length), F32),
+            jax.ShapeDtypeStruct((groups, length // n_seq), F32),
         ],
         scratch_shapes=[
             pltpu.VMEM(w_out.shape, BF16),
@@ -527,22 +585,22 @@
             pltpu.VMEM((groups, length), BF16),
             pltpu.VMEM((n_seq, groups, length), BF16),
             pltpu.VMEM((groups, 2 * rows), F32),
-            dma, dma((2,)), dma((2,)), dma((n_chan,)), dma((n_chan,)), dma((n_chan,)),
-            dma((n_chan,)), dma((n_seq,)), dma((n_seq,)), dma((n_seq,)), dma((n_seq,)),
-            dma((n_seq,)), dma((n_seq,)), dma((2, hops)), dma((2, hops)), dma((2, hops)),
-            dma((2, hops)),
+            pltpu.VMEM((groups, length), F32),
+            pltpu.VMEM((groups, length), F32),
+            pltpu.VMEM((rows, 2 * rows), F32),
+            pltpu.VMEM((rows, 2 * rows), F32),
+            pltpu.VMEM((rows, 2 * rows), F32),
+            dma, dma((2, chunks)), dma((2, chunks)), dma((n_chan,)), dma((n_chan,)),
+            dma((n_chan,)), dma((n_chan,)), dma((n_chan,)), dma((n_chan,)), dma((n_seq,)),
+            dma((n_seq,)), dma((n_seq,)), dma((n_seq,)), dma((n_seq,)), dma((n_seq,)),
+            dma((2, hops, chunks)), dma((2, hops, chunks)), dma((2, hops, chunks)),
+            dma((2, hops, chunks)),
         ],
         compiler_params=pltpu.CompilerParams(
             collective_id=0, has_side_effects=True, vmem_limit_bytes=56 * 2**20
         ),
-    )(
-        query_in, key_in, value_in, cotangent, fore_taps, back_taps, fmask, jnp.flip(fmask, 0),
-        bmask, w_out,
-    )
-    share = length // n_seq
-    at = length - (lax.axis_index("seq") + 1) * share
-    tap_sum = jnp.flip(lax.dynamic_slice_in_dim(taps, at, share, axis=1), 1)
-    return (block_out, grad_query, grad_key, grad_value, weight, tap_sum)
+    )(query_in, key_in, value_in, cotangent, filters, doc_lengths, w_out)
+    return tuple(results)
 
 
 def program(n_seq, n_chan, *arrays):

time: 106 us -> 91.1 us (0.86)
  the two profiles are of different devices: /device:TPU:4 before, /device:TPU:0 now
where the time goes in v3:
time: 91.1 us; the launch traced here: 90.8 us
  Pallas kernels  80 us (88%)
  local copies, waits for them, and re-layouts  10.1 us (11%)
    pallas_call x1, Pallas kernels, fused_body(): pl.pallas_call(functools.partial(mega_kernel, per_group, n_seq, n_chan, c...  80 us
    unnamed x7, local copies, waits for them, and re-layouts  8.47 us

profile of v3, /device:TPU:0, one launch (start us, length us, event | category | flops | bytes accessed | tf_op | source)
XLA Modules:
  0.0 90.8 jit_solution(8253495686585189968)
XLA Ops:
  0.6 80.0 %shard_map.118 = (bf16[128,1536]{1,0:T(8,128)(2,1)}, bf16[128,1536]{1,0:T(8,128)(2,1)}, bf16[128,1536]{1,0:T(8,128)(2,1)}, bf16[128,1536]{1,0:T(8,128)(2,1)}, bf...) custom-call(bf16[128,1536]{1,0:T(8,128)(2,1)} %q_ref.1, bf16[128,1536]{1,0:T(8,128)(2,1)} %k_ref.1, bf16[128,1536]{1,0:T(8,128)(2,1)} %v_ref.1, ...), custom_call_target="tpu_custom_call" | custom-call | tf_op jit(solution)/shard_map/pallas_call | solution.py:562
  80.7 0.0 copy-start
  80.7 1.6 %copy.13 = f32[96,16]{0,1:T(8,128)} copy(f32[96,16]{1,0:T(8,128)} %get-tuple-element.11) | data formatting | bytes 12288 | tf_op jit(solution)/shard_map/pallas_call | solution.py:562
  82.3 1.8 %copy.19 = bf16[128,1536]{1,0:T(8,128)(2,1)} copy(bf16[128,1536]{1,0:T(8,128)(2,1)} %get-tuple-element.18) | data formatting | bytes 786432
  84.1 1.8 %copy.20 = bf16[128,1536]{1,0:T(8,128)(2,1)} copy(bf16[128,1536]{1,0:T(8,128)(2,1)} %get-tuple-element.19) | data formatting | bytes 786432
  85.8 1.8 %copy.21 = bf16[128,1536]{1,0:T(8,128)(2,1)} copy(bf16[128,1536]{1,0:T(8,128)(2,1)} %get-tuple-element.20) | data formatting | bytes 786432
  87.6 1.8 %copy.22 = bf16[128,1536]{1,0:T(8,128)(2,1)} copy(bf16[128,1536]{1,0:T(8,128)(2,1)} %get-tuple-element.21) | data formatting | bytes 786432
  89.4 0.0 copy-done
  89.4 1.4 %copy.23 = bf16[1536,768]{1,0:T(8,128)(2,1)} copy(bf16[1536,768]{1,0:T(8,128)(2,1)S(1)} %copy-done) | data formatting | bytes 4718592
Async XLA Ops:
  80.7 8.7 %copy-start = (bf16[1536,768]{1,0:T(8,128)(2,1)S(1)}, bf16[1536,768]{1,0:T(8,128)(2,1)}, u32[]{:S(2)}) copy-start(bf16[1536,768]{1,0:T(8,128)(2,1)} %get-tuple-element.22) | copy-start | bytes 7077892

commit v4 on v3

--- a/solution.py
+++ b/solution.py
@@ -164,7 +164,8 @@
     per_group, n_seq, n_chan, chunks, q_ref, k_ref, v_ref, cot_ref, taps_ref, len_ref, w_hbm,
     out_ref, gq_ref, gk_ref, gv_ref, gw_ref, tap_ref,
     w_ref, kv_ref, prev_ref, gate_ref, next_ref, filt_ref, gin_ref, gall_ref, cots_ref, cotc_ref,
-    psend_ref, precv_ref, tsend_ref, trecv_ref, sums_ref, fore_ref, back_ref, fmask_ref, rmask_ref, bmask_ref,
+    psend_ref, precv_ref, tsend_ref, trecv_ref, sums_ref, fore_ref, back_ref, fmask_ref, rmask_ref,
+    bmask_ref,
     w_sem, rim_send, rim_recv, cot_send, cot_recv, pass_send, pass_recv, part_send, part_recv,
     a2a_send, a2a_recv, share_send, share_recv, tap_send, tap_recv, line_send, line_recv,
     pair_send, pair_recv,
@@ -173,7 +174,7 @@
     span = 2 * rows
     block = gw_ref.shape[1]
     per_chan = width // block
-    half = rows // 2
+    share_rows = rows // n_chan
     per_tile = LANES // per_group
     piece = width // chunks
     piece_tiles = piece // LANES
@@ -183,7 +184,6 @@
     z = s // 2
     pair = s + 1 - 2 * (s % 2)
     mate = c + 1 - 2 * (c % 2)
-    core = c % 2
 
     def remote(src, dst, send, recv, seq, chan):
         return pltpu.make_async_remote_copy(
@@ -267,18 +267,50 @@
 
     own_rows = pl.ds(pl.multiple_of(s * rows, rows), rows)
 
-    def line(side, h, ch, seq):
+    def line(side, h, ch, seq, other=0):
         rows_of = pl.ds(pl.multiple_of(seq * rows, rows), rows)
         part = gall_ref.at[rows_of, pl.ds(ch * piece, piece)]
         to = s + 2 if side == 0 else s - 2
-        return remote(part, part, line_send.at[side, h, ch], line_recv.at[side, h, ch], to, c)
+        at = h + other * hops
+        return remote(part, part, line_send.at[side, at, ch], line_recv.at[side, at, ch], to, c)
 
     def across(side, h, ch, seq):
         rows_of = pl.ds(pl.multiple_of(seq * rows, rows), rows)
         part = gall_ref.at[rows_of, pl.ds(ch * piece, piece)]
         return remote(part, part, pair_send.at[side, h, ch], pair_recv.at[side, h, ch], pair, c)
 
+    def pass_both(h, other):
+        base = pair if other else s
+        up, down = base - 2 * h, base + 2 * h
+        if h == 0 and other:
+            across(0, 0, 0, s).wait_recv()
+        if h > 0:
+            @pl.when(z - h >= 0)
+            def _():
+                line(0, h - 1, 0, up, other).wait_recv()
+
+        @pl.when((z - h >= 0) & (z < hops - 1))
+        def _():
+            line(0, h, 0, up, other).start()
+
+        if h > 0:
+            @pl.when(z + h < hops)
+            def _():
+                line(1, h - 1, 0, down, other).wait_recv()
+
+        @pl.when((z + h < hops) & (z > 0))
+        def _():
+            line(1, h, 0, down, other).start()
+
     def pass_on(h, ch):
+        if ch == 0:
+            if h == 0:
+                across(0, 0, 0, s).start()
+                pass_both(0, 0)
+            else:
+                pass_both(h, 0)
+                pass_both(h, 1)
+            return
         up, down = s - 2 * h, s + 2 * h
         if h > 0:
             @pl.when(z - h >= 0)
@@ -328,6 +360,8 @@
             gall_ref[own_rows, cols] = (q_ref[:, cols].astype(F32) * acc).astype(BF16)
 
         pass_on(0, ch)
+        if ch == min(1, chunks - 1):
+            pass_both(0, 1)
 
     for o in range(1, chips):
         cot_copy(o).wait_recv()
@@ -339,11 +373,12 @@
 
     def a2a_copy(o):
         to = lax.rem(s + o, n_seq)
-        half_rows = pl.ds(pl.multiple_of(core * half, half), half)
+        my_rows = pl.ds(pl.multiple_of(c * share_rows, share_rows), share_rows)
         src = cots_ref.at[
-            to // per_chan, half_rows, pl.ds(pl.multiple_of((to % per_chan) * block, block), block)
+            to // per_chan, my_rows, pl.ds(pl.multiple_of((to % per_chan) * block, block), block)
         ]
-        dst = cotc_ref.at[pl.ds(pl.multiple_of(s * rows + core * half, half), half), :]
+        at = pl.multiple_of(s * rows + c * share_rows, share_rows)
+        dst = cotc_ref.at[pl.ds(at, share_rows), :]
         return remote(src, dst, a2a_send.at[o], a2a_recv.at[o], to, c)
 
     for o in range(1, n_seq):
@@ -403,11 +438,13 @@
     for left in waiting:
         pass_on(*left)
 
-    def share_copy(o):
+    def share_copy(o, peer):
         came = lax.rem(s + n_seq - o, n_seq)
-        at = pl.ds(pl.multiple_of(came * rows + core * half, half), half)
+        at = pl.multiple_of(came * rows + c * share_rows, share_rows)
+        part = cotc_ref.at[pl.ds(at, share_rows), :]
         return remote(
-            cotc_ref.at[at, :], cotc_ref.at[at, :], share_send.at[o], share_recv.at[o], s, mate
+            part, part, share_send.at[o, peer], share_recv.at[o, peer], s,
+            lax.rem(c + peer, n_chan),
         )
 
     waiting = later[chunks:]
@@ -466,7 +503,8 @@
 
     for o in range(1, n_seq):
         a2a_copy(o).wait_recv()
-        share_copy(o).start()
+        for peer in range(1, n_chan):
+            share_copy(o, peer).start()
 
     for o in range(1, n_chan):
         part_copy(o).wait_recv()
@@ -489,9 +527,10 @@
     tap_ref[...] = total[:, :share]
 
     for o in range(1, n_seq):
-        share_copy(o).wait_recv()
+        for peer in range(1, n_chan):
+            share_copy(o, peer).wait_recv()
     for ch in range(chunks):
-        for h in range(hops):
+        for h in range(hops if ch else 0):
             @pl.when(z - h >= 0)
             def _():
                 across(0, h, ch, s - 2 * h).wait_recv()
@@ -526,10 +565,23 @@
         part_copy(o).wait_send()
     for o in range(1, n_seq):
         a2a_copy(o).wait_send()
-        share_copy(o).wait_send()
+        for peer in range(1, n_chan):
+            share_copy(o, peer).wait_send()
         tap_copy(o).wait_send()
+    across(0, 0, 0, s).wait_send()
     for h in range(hops):
-        for ch in range(chunks):
+        for other in range(2):
+            base = pair if other else s
+
+            @pl.when((z - h >= 0) & (z < hops - 1))
+            def _():
+                line(0, h, 0, base - 2 * h, other).wait_send()
+
+            @pl.when((z + h < hops) & (z > 0))
+            def _():
+                line(1, h, 0, base + 2 * h, other).wait_send()
+
+        for ch in range(1, chunks):
             @pl.when((z - h >= 0) & (z < hops - 1))
             def _():
                 line(0, h, ch, s - 2 * h).wait_send()
@@ -546,6 +598,23 @@
                 @pl.when(z + h < hops)
                 def _():
                     across(1, h, ch, s + 2 * h).wait_send()
+
+
+def hand_over(*refs):
+    big = (len(refs) - 4) // 3
+    ins, tap_in = refs[:big], refs[big]
+    outs, tap_out = refs[big + 1 : 2 * big + 1], refs[2 * big + 1]
+    held, in_sem, out_sem = refs[2 * big + 2 : 3 * big + 2], refs[-2], refs[-1]
+    loads = [pltpu.make_async_copy(ins[i], held[i], in_sem.at[i]) for i in range(big)]
+    stores = [pltpu.make_async_copy(held[i], outs[i], out_sem.at[i]) for i in range(big)]
+    for load in loads:
+        load.start()
+    tap_out[...] = tap_in[...]
+    for load, store in zip(loads, stores):
+        load.wait()
+        store.start()
+    for store in stores:
+        store.wait()
 
 
 def fused_body(n_seq, n_chan, query_in, key_in, value_in, filters, doc_lengths, w_out, cotangent):
@@ -592,15 +661,29 @@
             pltpu.VMEM((rows, 2 * rows), F32),
             dma, dma((2, chunks)), dma((2, chunks)), dma((n_chan,)), dma((n_chan,)),
             dma((n_chan,)), dma((n_chan,)), dma((n_chan,)), dma((n_chan,)), dma((n_seq,)),
-            dma((n_seq,)), dma((n_seq,)), dma((n_seq,)), dma((n_seq,)), dma((n_seq,)),
-            dma((2, hops, chunks)), dma((2, hops, chunks)), dma((2, hops, chunks)),
+            dma((n_seq,)), dma((n_seq, n_chan)), dma((n_seq, n_chan)), dma((n_seq,)),
+            dma((n_seq,)), dma((2, 2 * hops, chunks)), dma((2, 2 * hops, chunks)),
+            dma((2, hops, chunks)),
             dma((2, hops, chunks)),
         ],
         compiler_params=pltpu.CompilerParams(
             collective_id=0, has_side_effects=True, vmem_limit_bytes=56 * 2**20
         ),
     )(query_in, key_in, value_in, cotangent, filters, doc_lengths, w_out)
-    return tuple(results)
+    shapes = [jax.ShapeDtypeStruct(r.shape, r.dtype) for r in results]
+    hbm = pl.BlockSpec(memory_space=pl.ANY)
+    big = len(results) - 1
+    return tuple(
+        pl.pallas_call(
+            hand_over,
+            in_specs=[hbm] * big + [vmem],
+            out_specs=[hbm] * big + [vmem],
+            out_shape=shapes,
+            scratch_shapes=[pltpu.VMEM(r.shape, r.dtype) for r in shapes[:big]]
+            + [dma((big,)), dma((big,))],
+            compiler_params=pltpu.CompilerParams(vmem_limit_bytes=56 * 2**20),
+        )(*results)
+    )
 
 
 def program(n_seq, n_chan, *arrays):
@@ -608,7 +691,7 @@
     groups, length = arrays[3].shape
     block = arrays[5].shape[1] // n_seq
     aligned = block % LANES == 0 and width % block == 0 and width % (2 * LANES) == 0
-    even = n_seq % 2 == 0 and n_chan % 2 == 0 and n_seq >= 4
+    even = n_seq % 2 == 0 and n_chan % 2 == 0 and n_seq >= 4 and rows % (16 * n_chan) == 0
     if aligned and even and rows == length == LANES and LANES * groups % width == 0:
         return fused_body(n_seq, n_chan, *arrays)
     return body(n_seq, *arrays)

time: 91.1 us -> 98.5 us (1.081)
  Pallas kernels: 80 us -> 96.1 us
  local copies, waits for them, and re-layouts: 10.1 us -> 1.47 us
    pallas_call x1, Pallas kernels: 80 us -> 90.6 us  [fused_body(): pl.pallas_call(functools.partial(mega_kernel, per_group, n_seq, n_chan, c...]
    unnamed x7 -> x0, local copies, waits for them, and re-layouts: 8.47 us -> none
    pallas_call x0 -> x1, Pallas kernels: none -> 5.49 us  [fused_body(): pl.pallas_call(hand_over, in_specs=[hbm] * big + [vmem], out_specs=[hbm]...]
where the time goes in v4:
time: 98.5 us; the launch traced here: 98.3 us
  Pallas kernels  96.1 us (98%)
  local copies, waits for them, and re-layouts  1.47 us (1%)
    pallas_call x1, Pallas kernels, fused_body(): pl.pallas_call(functools.partial(mega_kernel, per_group, n_seq, n_chan, c...  90.6 us
    pallas_call x1, Pallas kernels, fused_body(): pl.pallas_call(hand_over, in_specs=[hbm] * big + [vmem], out_specs=[hbm]...  5.49 us

profile of v4, /device:TPU:0, one launch (start us, length us, event | category | flops | bytes accessed | tf_op | source)
XLA Modules:
  0.0 98.3 jit_solution(13338513058762265117)
XLA Ops:
  0.6 90.6 %shard_map.118 = (bf16[128,1536]{1,0:T(8,128)(2,1)}, bf16[128,1536]{1,0:T(8,128)(2,1)}, bf16[128,1536]{1,0:T(8,128)(2,1)}, bf16[128,1536]{1,0:T(8,128)(2,1)}, bf...) custom-call(bf16[128,1536]{1,0:T(8,128)(2,1)} %q_ref.1, bf16[128,1536]{1,0:T(8,128)(2,1)} %k_ref.1, bf16[128,1536]{1,0:T(8,128)(2,1)} %v_ref.1, ...), custom_call_target="tpu_custom_call" | custom-call | tf_op jit(solution)/shard_map/pallas_call | solution.py:631
  91.3 5.5 %shard_map.119 = (bf16[128,1536]{1,0:T(8,128)(2,1)}, bf16[128,1536]{1,0:T(8,128)(2,1)}, bf16[128,1536]{1,0:T(8,128)(2,1)}, bf16[128,1536]{1,0:T(8,128)(2,1)}, bf...) custom-call(bf16[128,1536]{1,0:T(8,128)(2,1)} %get-tuple-element.12.refs_0_, bf16[128,1536]{1,0:T(8,128)(2,1)} %get-tuple-element.13.refs_1_, ...), custom_call_target="tpu_custom_call" | custom-call | tf_op jit(solution)/shard_map/pallas_call | solution.py:677
  96.8 1.5 %copy.13 = f32[96,16]{0,1:T(8,128)} copy(f32[96,16]{1,0:T(8,128)} %get-tuple-element.23) | data formatting | bytes 12288 | tf_op jit(solution)/shard_map/pallas_call | solution.py:677

commit v5 on v3

--- a/solution.py
+++ b/solution.py
@@ -164,8 +164,8 @@
     per_group, n_seq, n_chan, chunks, q_ref, k_ref, v_ref, cot_ref, taps_ref, len_ref, w_hbm,
     out_ref, gq_ref, gk_ref, gv_ref, gw_ref, tap_ref,
     w_ref, kv_ref, prev_ref, gate_ref, next_ref, filt_ref, gin_ref, gall_ref, cots_ref, cotc_ref,
-    psend_ref, precv_ref, tsend_ref, trecv_ref, sums_ref, fore_ref, back_ref, fmask_ref, rmask_ref, bmask_ref,
-    w_sem, rim_send, rim_recv, cot_send, cot_recv, pass_send, pass_recv, part_send, part_recv,
+    psend_ref, precv_ref, tsend_ref, trecv_ref, sums_ref, fore_ref, back_ref, fmask_ref, rmask_ref,
+    bmask_ref, cott_ref, turned_ref, w_sem, rim_send, rim_recv, cot_send, cot_recv, pass_send, pass_recv, part_send, part_recv,
     a2a_send, a2a_recv, share_send, share_recv, tap_send, tap_recv, line_send, line_recv,
     pair_send, pair_recv,
 ):
@@ -349,21 +349,17 @@
     for o in range(1, n_seq):
         a2a_copy(o).start()
 
+    for p in range(n_chan):
+        cott_ref[p * width : (p + 1) * width, :] = cots_ref[p].T
+
     in_tile = 2 * LANES
     piece_ins = piece // in_tile
 
     for ch in range(chunks):
-        @pl.loop(ch * piece_ins, (ch + 1) * piece_ins)
-        def _(tile):
-            cols = pl.ds(pl.multiple_of(tile * in_tile, in_tile), in_tile)
-            acc = jnp.zeros((rows, in_tile), F32)
-            for p in range(n_chan):
-                acc = acc + lax.dot_general(
-                    cots_ref[p], w_ref[cols, p * width : (p + 1) * width],
-                    (((1,), (1,)), ((), ())), preferred_element_type=F32,
-                )
-            gin_ref[:, cols] = acc
-            gate_ref[:, cols] = (acc * q_ref[:, cols].astype(F32)).astype(BF16)
+        cols = pl.ds(ch * piece, piece)
+        acc = jnp.dot(w_ref[cols, :], cott_ref[...], preferred_element_type=F32).T
+        gin_ref[:, cols] = acc
+        gate_ref[:, cols] = (acc * q_ref[:, cols].astype(F32)).astype(BF16)
 
         @pl.when(s > 0)
         def _():
@@ -484,9 +480,9 @@
     total = trecv_ref[0].astype(F32)
     for p in range(1, n_seq):
         total = total + trecv_ref[p].astype(F32)
-    share = tap_ref.shape[1]
-    total = pltpu.roll(total, lax.rem(LANES - s * share, LANES), 1)
-    tap_ref[...] = total[:, :share]
+    share = tap_ref.shape[0]
+    turned_ref[...] = total.T
+    tap_ref[...] = turned_ref[pl.ds(pl.multiple_of(s * share, share), share), :]
 
     for o in range(1, n_seq):
         share_copy(o).wait_recv()
@@ -546,6 +542,23 @@
                 @pl.when(z + h < hops)
                 def _():
                     across(1, h, ch, s + 2 * h).wait_send()
+
+
+def hand_over(*refs):
+    big = (len(refs) - 4) // 3
+    ins, tap_in = refs[:big], refs[big]
+    outs, tap_out = refs[big + 1 : 2 * big + 1], refs[2 * big + 1]
+    held, in_sem, out_sem = refs[2 * big + 2 : 3 * big + 2], refs[-2], refs[-1]
+    loads = [pltpu.make_async_copy(ins[i], held[i], in_sem.at[i]) for i in range(big)]
+    stores = [pltpu.make_async_copy(held[i], outs[i], out_sem.at[i]) for i in range(big)]
+    for load in loads:
+        load.start()
+    tap_out[...] = tap_in[...]
+    for load, store in zip(loads, stores):
+        load.wait()
+        store.start()
+    for store in stores:
+        store.wait()
 
 
 def fused_body(n_seq, n_chan, query_in, key_in, value_in, filters, doc_lengths, w_out, cotangent):
@@ -567,7 +580,7 @@
         out_shape=[act] * 4
         + [
             jax.ShapeDtypeStruct((width, block), BF16),
-            jax.ShapeDtypeStruct((groups, length // n_seq), F32),
+            jax.ShapeDtypeStruct((length // n_seq, groups), F32),
         ],
         scratch_shapes=[
             pltpu.VMEM(w_out.shape, BF16),
@@ -590,6 +603,8 @@
             pltpu.VMEM((rows, 2 * rows), F32),
             pltpu.VMEM((rows, 2 * rows), F32),
             pltpu.VMEM((rows, 2 * rows), F32),
+            pltpu.VMEM((w_out.shape[1], rows), BF16),
+            pltpu.VMEM((length, groups), F32),
             dma, dma((2, chunks)), dma((2, chunks)), dma((n_chan,)), dma((n_chan,)),
             dma((n_chan,)), dma((n_chan,)), dma((n_chan,)), dma((n_chan,)), dma((n_seq,)),
             dma((n_seq,)), dma((n_seq,)), dma((n_seq,)), dma((n_seq,)), dma((n_seq,)),
@@ -600,7 +615,19 @@
             collective_id=0, has_side_effects=True, vmem_limit_bytes=56 * 2**20
         ),
     )(query_in, key_in, value_in, cotangent, filters, doc_lengths, w_out)
-    return tuple(results)
+    shapes = [jax.ShapeDtypeStruct(r.shape, r.dtype) for r in results]
+    hbm = pl.BlockSpec(memory_space=pl.ANY)
+    big = len(results) - 1
+    results = pl.pallas_call(
+        hand_over,
+        in_specs=[hbm] * big + [vmem],
+        out_specs=[hbm] * big + [vmem],
+        out_shape=shapes,
+        scratch_shapes=[pltpu.VMEM(r.shape, r.dtype) for r in shapes[:big]]
+        + [dma((big,)), dma((big,))],
+        compiler_params=pltpu.CompilerParams(vmem_limit_bytes=56 * 2**20),
+    )(*results)
+    return tuple(results[:big]) + (results[big].T,)
 
 
 def program(n_seq, n_chan, *arrays):
@@ -608,7 +635,7 @@
     groups, length = arrays[3].shape
     block = arrays[5].shape[1] // n_seq
     aligned = block % LANES == 0 and width % block == 0 and width % (2 * LANES) == 0
-    even = n_seq % 2 == 0 and n_chan % 2 == 0 and n_seq >= 4
+    even = n_seq % 2 == 0 and n_chan % 2 == 0 and n_seq >= 4 and length % (8 * n_seq) == 0
     if aligned and even and rows == length == LANES and LANES * groups % width == 0:
         return fused_body(n_seq, n_chan, *arrays)
     return body(n_seq, *arrays)

time: 91.1 us -> 86.3 us (0.947)
  local copies, waits for them, and re-layouts: 10.1 us -> 0 us
  Pallas kernels: 80 us -> 85.4 us
    unnamed x7 -> x0, local copies, waits for them, and re-layouts: 8.47 us -> none
    pallas_call x0 -> x1, Pallas kernels: none -> 5.37 us  [fused_body(): pl.pallas_call(hand_over, in_specs=[hbm] * big + [vmem], out_specs=[hbm]...]
    pallas_call x1 -> x0, local copies, waits for them, and re-layouts: 1.62 us -> none  [fused_body(): pl.pallas_call(functools.partial(mega_kernel, per_group, n_seq, n_chan, c...]
where the time goes in v5:
time: 86.3 us; the launch traced here: 86.1 us
  Pallas kernels  85.4 us (99%)
    pallas_call x1, Pallas kernels, fused_body(): pl.pallas_call(functools.partial(mega_kernel, per_group, n_seq, n_chan, c...  80 us
    pallas_call x1, Pallas kernels, fused_body(): pl.pallas_call(hand_over, in_specs=[hbm] * big + [vmem], out_specs=[hbm]...  5.37 us

profile of v5, /device:TPU:0, one launch (start us, length us, event | category | flops | bytes accessed | tf_op | source)
XLA Modules:
  0.0 86.1 jit_solution(13119931357540298513)
XLA Ops:
  0.6 80.0 %shard_map.118 = (bf16[128,1536]{1,0:T(8,128)(2,1)}, bf16[128,1536]{1,0:T(8,128)(2,1)}, bf16[128,1536]{1,0:T(8,128)(2,1)}, bf16[128,1536]{1,0:T(8,128)(2,1)}, bf...) custom-call(bf16[128,1536]{1,0:T(8,128)(2,1)} %q_ref.1, bf16[128,1536]{1,0:T(8,128)(2,1)} %k_ref.1, bf16[128,1536]{1,0:T(8,128)(2,1)} %v_ref.1, ...), custom_call_target="tpu_custom_call" | custom-call | tf_op jit(solution)/shard_map/pallas_call | solution.py:575
  80.7 5.4 %shard_map.119 = (bf16[128,1536]{1,0:T(8,128)(2,1)}, bf16[128,1536]{1,0:T(8,128)(2,1)}, bf16[128,1536]{1,0:T(8,128)(2,1)}, bf16[128,1536]{1,0:T(8,128)(2,1)}, bf...) custom-call(bf16[128,1536]{1,0:T(8,128)(2,1)} %get-tuple-element.18.refs_0_, bf16[128,1536]{1,0:T(8,128)(2,1)} %get-tuple-element.19.refs_1_, ...), custom_call_target="tpu_custom_call" | custom-call | tf_op jit(solution)/shard_map/pallas_call | solution.py:621

commit v6 on v5

--- a/solution.py
+++ b/solution.py
@@ -173,7 +173,7 @@
     span = 2 * rows
     block = gw_ref.shape[1]
     per_chan = width // block
-    half = rows // 2
+    share_rows = rows // n_chan
     per_tile = LANES // per_group
     piece = width // chunks
     piece_tiles = piece // LANES
@@ -183,7 +183,6 @@
     z = s // 2
     pair = s + 1 - 2 * (s % 2)
     mate = c + 1 - 2 * (c % 2)
-    core = c % 2
 
     def remote(src, dst, send, recv, seq, chan):
         return pltpu.make_async_remote_copy(
@@ -339,11 +338,12 @@
 
     def a2a_copy(o):
         to = lax.rem(s + o, n_seq)
-        half_rows = pl.ds(pl.multiple_of(core * half, half), half)
+        my_rows = pl.ds(pl.multiple_of(c * share_rows, share_rows), share_rows)
         src = cots_ref.at[
-            to // per_chan, half_rows, pl.ds(pl.multiple_of((to % per_chan) * block, block), block)
+            to // per_chan, my_rows, pl.ds(pl.multiple_of((to % per_chan) * block, block), block)
         ]
-        dst = cotc_ref.at[pl.ds(pl.multiple_of(s * rows + core * half, half), half), :]
+        at = pl.multiple_of(s * rows + c * share_rows, share_rows)
+        dst = cotc_ref.at[pl.ds(at, share_rows), :]
         return remote(src, dst, a2a_send.at[o], a2a_recv.at[o], to, c)
 
     for o in range(1, n_seq):
@@ -399,12 +399,19 @@
     for left in waiting:
         pass_on(*left)
 
-    def share_copy(o):
+    def share_copy(o, peer):
         came = lax.rem(s + n_seq - o, n_seq)
-        at = pl.ds(pl.multiple_of(came * rows + core * half, half), half)
+        at = pl.multiple_of(came * rows + c * share_rows, share_rows)
+        part = cotc_ref.at[pl.ds(at, share_rows), :]
         return remote(
-            cotc_ref.at[at, :], cotc_ref.at[at, :], share_send.at[o], share_recv.at[o], s, mate
-        )
+            part, part, share_send.at[o, peer], share_recv.at[o, peer], s,
+            lax.rem(c + peer, n_chan),
+        )
+
+    for o in range(1, n_seq):
+        a2a_copy(o).wait_recv()
+        for peer in range(1, n_chan):
+            share_copy(o, peer).start()
 
     waiting = later[chunks:]
     for ch in range(chunks):
@@ -460,10 +467,6 @@
         tap_copy(o).start()
     trecv_ref[s] = tsend_ref[...]
 
-    for o in range(1, n_seq):
-        a2a_copy(o).wait_recv()
-        share_copy(o).start()
-
     for o in range(1, n_chan):
         part_copy(o).wait_recv()
 
@@ -485,7 +488,8 @@
     tap_ref[...] = turned_ref[pl.ds(pl.multiple_of(s * share, share), share), :]
 
     for o in range(1, n_seq):
-        share_copy(o).wait_recv()
+        for peer in range(1, n_chan):
+            share_copy(o, peer).wait_recv()
     for ch in range(chunks):
         for h in range(hops):
             @pl.when(z - h >= 0)
@@ -522,7 +526,8 @@
         part_copy(o).wait_send()
     for o in range(1, n_seq):
         a2a_copy(o).wait_send()
-        share_copy(o).wait_send()
+        for peer in range(1, n_chan):
+            share_copy(o, peer).wait_send()
         tap_copy(o).wait_send()
     for h in range(hops):
         for ch in range(chunks):
@@ -607,7 +612,7 @@
             pltpu.VMEM((length, groups), F32),
             dma, dma((2, chunks)), dma((2, chunks)), dma((n_chan,)), dma((n_chan,)),
             dma((n_chan,)), dma((n_chan,)), dma((n_chan,)), dma((n_chan,)), dma((n_seq,)),
-            dma((n_seq,)), dma((n_seq,)), dma((n_seq,)), dma((n_seq,)), dma((n_seq,)),
+            dma((n_seq,)), dma((n_seq, n_chan)), dma((n_seq, n_chan)), dma((n_seq,)), dma((n_seq,)),
             dma((2, hops, chunks)), dma((2, hops, chunks)), dma((2, hops, chunks)),
             dma((2, hops, chunks)),
         ],
@@ -635,7 +640,7 @@
     groups, length = arrays[3].shape
     block = arrays[5].shape[1] // n_seq
     aligned = block % LANES == 0 and width % block == 0 and width % (2 * LANES) == 0
-    even = n_seq % 2 == 0 and n_chan % 2 == 0 and n_seq >= 4 and length % (8 * n_seq) == 0
+    even = n_seq % 2 == 0 and n_chan % 2 == 0 and n_seq >= 4 and rows % (16 * n_chan) == 0 and length % (8 * n_seq) == 0
     if aligned and even and rows == length == LANES and LANES * groups % width == 0:
         return fused_body(n_seq, n_chan, *arrays)
     return body(n_seq, *arrays)

time: 86.3 us -> 81.2 us (0.941)
  Pallas kernels: 85.4 us -> 80.1 us
    pallas_call x1, Pallas kernels: 80 us -> 74.7 us  [fused_body(): pl.pallas_call(functools.partial(mega_kernel, per_group, n_seq, n_chan, c...]
where the time goes in v6:
time: 81.2 us; the launch traced here: 80.7 us
  Pallas kernels  80.1 us (99%)
    pallas_call x1, Pallas kernels, fused_body(): pl.pallas_call(functools.partial(mega_kernel, per_group, n_seq, n_chan, c...  74.7 us
    pallas_call x1, Pallas kernels, fused_body(): pl.pallas_call(hand_over, in_specs=[hbm] * big + [vmem], out_specs=[hbm]...  5.37 us

profile of v6, /device:TPU:0, one launch (start us, length us, event | category | flops | bytes accessed | tf_op | source)
XLA Modules:
  0.0 80.7 jit_solution(14536800794170808554)
XLA Ops:
  0.6 74.7 %shard_map.118 = (bf16[128,1536]{1,0:T(8,128)(2,1)}, bf16[128,1536]{1,0:T(8,128)(2,1)}, bf16[128,1536]{1,0:T(8,128)(2,1)}, bf16[128,1536]{1,0:T(8,128)(2,1)}, bf...) custom-call(bf16[128,1536]{1,0:T(8,128)(2,1)} %q_ref.1, bf16[128,1536]{1,0:T(8,128)(2,1)} %k_ref.1, bf16[128,1536]{1,0:T(8,128)(2,1)} %v_ref.1, ...), custom_call_target="tpu_custom_call" | custom-call | tf_op jit(solution)/shard_map/pallas_call | solution.py:580
  75.4 5.4 %shard_map.119 = (bf16[128,1536]{1,0:T(8,128)(2,1)}, bf16[128,1536]{1,0:T(8,128)(2,1)}, bf16[128,1536]{1,0:T(8,128)(2,1)}, bf16[128,1536]{1,0:T(8,128)(2,1)}, bf...) custom-call(bf16[128,1536]{1,0:T(8,128)(2,1)} %get-tuple-element.18.refs_0_, bf16[128,1536]{1,0:T(8,128)(2,1)} %get-tuple-element.19.refs_1_, ...), custom_call_target="tpu_custom_call" | custom-call | tf_op jit(solution)/shard_map/pallas_call | solution.py:626
